TPU v7x, 128 devices: a whole 4x4x4 slice. The times are simulated.
128 devices in a mesh: group: 4 (over z), head: 32 (over y, x, core).
Axes of the slice: x: 4, y: 4, z: 4, core: 2. Of those that a mesh axis runs over, the one named last changes fastest.
Arguments:
- mixer_input: bfloat16 [4096, 16384], P('group', 'head'), may hold values from -6 to 6
- gate_input: bfloat16 [4096, 16384], P('group', 'head'), may hold values from -6 to 6
- step_raw: float32 [4096, 256], P('group', 'head'), may hold values from -5 to 5
- state_proj: bfloat16 [2, 4096, 8, 256], P(None, 'group'), may hold values from -0.75 to 0.75
- decay_log: float32 [256], P('head'), may hold values from -6.2 to -2.3
- step_bias: float32 [256], P('head'), may hold values from -2 to 0.5
- skip_gain: float32 [256], P('head'), may hold values from 0.3 to 2
- norm_gain: float32 [16384], P('head'), may hold values from 0.5 to 1.5
- out_weight: bfloat16 [16384, 8192], P('head'), may hold values from -0.09375 to 0.09375
- residual: bfloat16 [4096, 8192], P('group', 'head'), may hold values from -6 to 6
- new_spans: int32 [8], P('group'), may hold values from 1 to 4
- hit_owner: int32 [8, 256], P('group', 'head'), may hold values from 0 to 3, as said below
- hit_slot: int32 [8, 256], P('group', 'head'), may hold values from 0 to 7
- state_cache: bfloat16 [32, 256, 64, 256], P('group', 'head'), may hold values from -16 to 16
Outputs:
- mixed: bfloat16 [4096, 8192], P('group', 'head')
- final_state: float32 [8, 256, 64, 256], P('group', 'head')
Inputs may be any that keep to these rules, and one draw needn't show every extreme that they name: `hit_owner`: within the 2 x 8 block of one device (one index of group, one index of head), no owner is named by more than 6 entries, and one owner is named by exactly 6.
All inputs are finite; a program needn't handle non-finite values.
Results may differ from a plain program's by a relative error of at most 0.017.
Values may be sent and summed in bfloat16 or wider, within the bound.
A program may use at most 128 MiB of HBM per device.

v0:
```python
import jax
import jax.numpy as jnp
from jax import lax
from jax.sharding import PartitionSpec as P

SPAN = 128


def per_device(
    mixer_input,
    gate_input,
    step_raw,
    state_proj,
    decay_log,
    step_bias,
    skip_gain,
    norm_gain,
    out_weight,
    residual,
    new_spans,
    hit_owner,
    hit_slot,
    state_cache,
):
    highest = lax.Precision.HIGHEST
    session_count = new_spans.shape[0]
    head_count = decay_log.shape[0]
    row_count = mixer_input.shape[0]
    turn_length = row_count // session_count
    span_count = turn_length // SPAN
    head_width = mixer_input.shape[1] // head_count
    state_width = state_proj.shape[3]
    group_count = state_proj.shape[2]
    per_group = head_count * lax.axis_size("head") // group_count
    group_index = lax.axis_index("head") * head_count // per_group
    block_count = session_count * head_count
    owners = hit_owner.reshape(block_count)
    slot_index = hit_slot.reshape(block_count)
    local_head = jnp.arange(block_count, dtype=jnp.int32) % head_count
    flat_width = head_width * state_width
    every_cache = lax.all_gather(state_cache, "group", axis=0, tiled=True)
    slot_count = state_cache.shape[0]
    flat_cache = every_cache.reshape(-1, flat_width)
    wanted = (owners * slot_count + slot_index) * head_count + local_head
    fetched = jnp.take(flat_cache, wanted, axis=0)
    start_state = fetched.astype(jnp.float32).reshape(
        session_count, head_count, head_width, state_width
    )
    live = (jnp.arange(turn_length, dtype=jnp.int32)[None, :] < (new_spans * SPAN)[:, None]).astype(
        jnp.float32
    )
    steps = (
        jax.nn.softplus(step_raw.reshape(session_count, turn_length, head_count) + step_bias)
        * live[:, :, None]
    )
    rates = -jnp.exp(decay_log) * steps
    shape_four = (session_count, span_count, SPAN, head_count)
    steps = steps.reshape(shape_four)
    cumulative = jnp.cumsum(rates.reshape(shape_four), axis=2)
    values = mixer_input.reshape(session_count, span_count, SPAN, head_count, head_width)
    inputs_b = lax.dynamic_index_in_dim(state_proj[0], group_index, 1, keepdims=False)
    inputs_b = inputs_b.reshape(session_count, span_count, SPAN, state_width)
    outputs_c = lax.dynamic_index_in_dim(state_proj[1], group_index, 1, keepdims=False)
    outputs_c = outputs_c.reshape(session_count, span_count, SPAN, state_width)
    lower = jnp.arange(SPAN)[:, None] >= jnp.arange(SPAN)[None, :]

    def span_step(carried, inputs):
        values_c, inputs_c, reads_c, steps_c, cumul_c = inputs
        scores = jnp.einsum("stn,sun->stu", reads_c, inputs_c, preferred_element_type=jnp.float32)
        differ = cumul_c[:, :, None] - cumul_c[:, None, :]
        weights = jnp.where(lower[None, :, :, None], jnp.exp(jnp.minimum(differ, 0.0)), 0.0)
        weights = (weights * scores[..., None] * steps_c[:, None]).astype(jnp.bfloat16)
        within = jnp.einsum(
            "stuh,suhp->sthp", weights, values_c, preferred_element_type=jnp.float32
        )
        carried_in = (
            jnp.einsum("stn,shpn->sthp", reads_c.astype(jnp.float32), carried, precision=highest)
            * jnp.exp(cumul_c)[..., None]
        )
        to_end = jnp.exp(cumul_c[:, -1:] - cumul_c) * steps_c
        scaled = (to_end[..., None] * values_c.astype(jnp.float32)).astype(jnp.bfloat16)
        update = jnp.einsum("suhp,sun->shpn", scaled, inputs_c, preferred_element_type=jnp.float32)
        carried_next = jnp.exp(cumul_c[:, -1])[..., None, None] * carried + update
        result = within + carried_in + skip_gain[None, None, :, None] * values_c.astype(jnp.float32)
        return (carried_next, result)

    scanned = tuple(
        (jnp.moveaxis(member, 1, 0) for member in (values, inputs_b, outputs_c, steps, cumulative))
    )
    carried_final, outputs = lax.scan(span_step, start_state, scanned)
    outputs = jnp.moveaxis(outputs, 0, 1).reshape(row_count, head_count * head_width)
    gated = outputs * jax.nn.silu(gate_input.astype(jnp.float32))
    squares = jnp.sum(gated * gated, axis=1)
    totals = lax.psum(squares, "head")
    inner_width = head_count * head_width * lax.axis_size("head")
    scaling = lax.rsqrt(totals / inner_width + 1e-05)
    normed = (gated * scaling[:, None] * norm_gain).astype(jnp.bfloat16)
    partial_out = jnp.dot(normed, out_weight, preferred_element_type=jnp.float32)
    term = lax.optimization_barrier(partial_out.astype(jnp.bfloat16)).astype(jnp.float32)
    summed = lax.psum_scatter(
        term.astype(jnp.bfloat16), "head", scatter_dimension=1, tiled=True
    ).astype(jnp.float32)
    mixed = (residual.astype(jnp.float32) + summed).astype(jnp.bfloat16)
    return (mixed, carried_final)


def solution(mesh):
    in_specs = (
        P("group", "head"),
        P("group", "head"),
        P("group", "head"),
        P(None, "group", None, None),
        P("head"),
        P("head"),
        P("head"),
        P("head"),
        P("head", None),
        P("group", "head"),
        P("group"),
        P("group", "head"),
        P("group", "head"),
        P("group", "head", None, None),
    )
    out_specs = (P("group", "head"), P("group", "head", None, None))
    return jax.shard_map(
        per_device, mesh=mesh, in_specs=in_specs, out_specs=out_specs, check_vma=False
    )
```

profile of v0, /device:TPU:1, one launch (start us, length us, event | category | flops | bytes accessed | tf_op | source)
XLA Modules:
  0.0 355.1 jit_solution(6096453827277040406)
XLA Ops:
  8.6 1.3 copy.57
  11.5 3.8 %fusion.48 = (bf16[1,1024,8,256]{3,2,1,0:T(8,128)(2,1)S(1)}, bf16[1,1024,8,256]{3,2,1,0:T(8,128)(2,1)S(1)}) fusion(bf16[2,1024,8,256]{3,2,1,0:T(8,128)(2,1)} %param.19), kind=kLoop, calls=%fused_computation.81 | loop fusion | bytes 16777216 | tf_op jit(solution)/shard_map/slice | solution.py:63
  15.3 2.2 constant_dynamic-slice_fusion.2
  18.4 1.2 reduce_window_sum.11
  19.7 76.6 %all-gather.2.cloned.1.call-done = bf16[32,8,64,256]{3,2,1,0:T(8,128)(2,1)} async-done(((bf16[8,8,64,256]{3,2,1,0:T(8,128)(2,1)}), bf16[32,8,64,256]{3,2,1,0:T(8,128)(2,1)}) %all-gather.2.cloned.1.call-update) | async-done | bytes 8388624 | tf_op jit(solution)/shard_map/all_gather | solution.py:41
  96.3 15.3 %copy.68 = bf16[32,8,64,256]{3,1,2,0:T(8,128)(2,1)} copy(bf16[32,8,64,256]{3,2,1,0:T(8,128)(2,1)} %all-gather.2.cloned.1.call-done) | data formatting | bytes 16777216
  111.6 6.0 %gather_fusion = bf16[16,16384]{1,0:T(8,128)(2,1)S(1)} fusion(bf16[256,16384]{1,0:T(8,128)(2,1)} %bitcast.104, s32[1024]{0:T(1024)S(1)} %pad_clamp_fusion), kind=kCustom, calls=%fused_computation | custom fusion | bytes 1048640 | tf_op jit(solution)/shard_map/jit(_take)/gather | solution.py:45
  117.7 25.0 %while.13 = (s32[]{:T(128)}, f32[2,8,64,256]{3,2,1,0:T(8,128)S(1)}, f32[4,2,128,8,64]{2,4,3,1,0:T(8,128)}, f32[4,2,128,8]{3,2,0,1:T(8,128)}, f32[4,2,128,8]{2,3,...) while((s32[]{:T(128)}, f32[2,8,64,256]{3,2,1,0:T(8,128)S(1)}, ...), condition=%wide.region_2.3_spmd.clone, body=%wide.region_1.2_spmd.clone.sunk | while | flops 523259904 | bytes 6534073 | solution.py:90
  121.1 1.4 fusion.72
  122.6 1.4 convolution_add_fusion.2
  125.7 1.1 fusion.71
  127.4 1.4 fusion.72
  128.8 1.4 convolution_add_fusion.2
  133.6 1.5 fusion.72
  135.1 1.4 convolution_add_fusion.2
  139.9 1.4 fusion.72
  141.3 1.4 convolution_add_fusion.2
  142.8 4.7 %copy.56 = f32[2,4,128,8,64]{2,1,0,4,3:T(4,128)} copy(f32[2,4,128,8,64]{2,4,3,0,1:T(8,128)} %bitcast.113) | data formatting | bytes 4194304 | tf_op jit(solution)/shard_map/transpose | solution.py:91
  147.4 3.2 reshape.177
  150.6 2.6 multiply_reduce_fusion
  153.1 62.7 %psum.7 = f32[1024]{0:T(1024)S(1)} all-reduce(f32[1024]{0:T(1024)S(1)} %multiply_reduce_fusion), channel_id=1, replica_groups=mesh['group'=4,'head'=32] {'head'}, use_global_device_ids=true, to_apply=%region_4.5 | all-reduce | flops 1024 | bytes 8192 | tf_op jit(solution)/shard_map/psum | solution.py:94
  215.9 16.1 %convolution_convert_fusion = bf16[1024,8192]{1,0:T(8,128)(2,1)} fusion(bf16[512,8192]{1,0:T(8,128)(2,1)} %param.24, f32[512]{0:T(512)S(1)} %copy-done.11, f32[1024]{0:T(1024)S(1)} %add_rsqrt_fusion, f32[1024,512]{0,1:T(8,128)S(1)} %copy-done.1, bf16[1024,512]{0,1:T(8,128)(2,1)S(1)} %copy-done.2), kind=kOutput, calls=%fused_computation.46 | convolution fusion | flops 8603041792 | bytes 28317696 | tf_op jit(solution)/shard_map/dot_general | solution.py:98
  232.0 114.3 %reduce-scatter.2.cloned.1.call-done = bf16[1024,256]{1,0:T(8,128)(2,1)} async-done(((bf16[1024,8192]{1,0:T(8,128)(2,1)}), bf16[1024,256]{1,0:T(8,128)(2,1)}) %reduce-scatter.2.cloned.1.call-update) | async-done | bytes 524304 | tf_op jit(solution)/shard_map/reduce_scatter | solution.py:100
  346.3 2.0 add_convert_fusion
  (105 shorter events, 16.2 us)
Async XLA Ops:
  7.2 0.9 copy-start.8
  7.2 0.9 copy-start.9
  7.2 1.0 copy-start.12
  7.2 1.0 copy-start.13
  7.2 1.1 copy-start.10
  7.2 1.1 copy-start.6
  7.2 1.4 copy-start.3
  7.2 2.7 copy-start.4
  7.2 89.1 %all-gather.2.cloned.1.call-start = ((), (), s32[]{:S(2)}) async-start(), calls=%async_computation.1 | async-start | bytes 10485760 | tf_op jit(solution)/shard_map/all_gather | solution.py:41
  8.0 338.3 %reduce-scatter.2.cloned.1.call-start = ((), (), s32[]{:S(2)}) async-start(), calls=%async_computation.2 | async-start | bytes 17301504 | tf_op jit(solution)/shard_map/reduce_scatter | solution.py:100
  111.6 6.2 %copy-start.7 = (f32[8]{0:T(128)S(1)}, f32[8]{0:T(128)}, u32[]{:S(2)}) copy-start(f32[8]{0:T(128)} %param.22) | copy-start | bytes 100
  142.7 4.7 %copy-start = (f32[2,8,64,256]{3,2,1,0:T(8,128)}, f32[2,8,64,256]{3,2,1,0:T(8,128)S(1)}, u32[]{:S(2)}) copy-start(f32[2,8,64,256]{3,2,1,0:T(8,128)S(1)} %get-tuple-element.54) | copy-start | bytes 3145732
  147.4 3.2 copy-start.2
  150.6 65.3 %copy-start.1 = (f32[1024,512]{0,1:T(8,128)S(1)}, f32[1024,512]{0,1:T(8,128)}, u32[]{:S(2)}) copy-start(f32[1024,512]{0,1:T(8,128)} %reshape.177) | copy-start | bytes 6291460
  150.6 65.3 %copy-start.11 = (f32[512]{0:T(512)S(1)}, f32[512]{0:T(512)}, u32[]{:S(2)}) copy-start(f32[512]{0:T(512)} %param.23) | copy-start | bytes 6148
  232.0 114.3 %copy-start.5 = (bf16[1024,256]{1,0:T(8,128)(2,1)S(1)}, bf16[1024,256]{1,0:T(8,128)(2,1)}, u32[]{:S(2)}) copy-start(bf16[1024,256]{1,0:T(8,128)(2,1)} %param.25) | copy-start | bytes 1572868
Sparse Core Ops, SparseCore 0:
  9.7 86.5 all-gather.1
  232.1 114.0 reduce-scatter.1
where the time goes:
time: 356 us; the launch traced here: 355 us
  waiting for transfers between devices  192 us (54%)
  blocking collectives  62.7 us (18%)
  local copies, waits for them, and re-layouts  45 us (13%)
  matrix products  34.1 us (10%)
  between operations  14.3 us (4%)
  other arithmetic  7.01 us (2%)
    reduce_scatter x1, waiting for transfers between devices, per_device(): lax.psum_scatter(term.astype(jnp.bfloat16), 'head', scatter_dimension=1,...  114 us
    all_gather x1, waiting for transfers between devices, per_device(): every_cache = lax.all_gather(state_cache, 'group', axis=0, tiled=True)  76.6 us
    psum x1, blocking collectives, per_device(): totals = lax.psum(squares, 'head')  62.7 us
    unnamed x34, local copies, waits for them, and re-layouts  18.4 us
    dot_general x1, matrix products, per_device(): jnp.dot(normed, out_weight, preferred_element_type=jnp.float32)  16.1 us
  transfers between devices with their start and end apart: 2, of which 2 were waited for; matrix products, arithmetic and copies ran while one was open for 3% of the time, Pallas kernels for 0%

commit v1 on v0

--- a/solution.py
+++ b/solution.py
@@ -1,9 +1,275 @@
 import jax
 import jax.numpy as jnp
 from jax import lax
+from jax.experimental import pallas as pl
+from jax.experimental.pallas import tpu as pltpu
 from jax.sharding import PartitionSpec as P
 
 SPAN = 128
+
+HALF = (0, 1)
+ORDER = ((2, 0), (2, 1), (0, 2), (1, 2), (2, 2), (2, 3), (3, 2), (1, 3), (3, 0), (3, 1), (0, 3), (1, 0), (1, 1), (3, 3), (0, 1), (0, 0))
+SIDE = 4
+CHUNKS = 4
+MESH = pl.DeviceIdType.MESH
+BF16 = jnp.bfloat16
+F32 = jnp.float32
+
+
+def remote(src, dst, send_sem, recv_sem, head):
+    return pltpu.make_async_remote_copy(
+        src_ref=src, dst_ref=dst, send_sem=send_sem, recv_sem=recv_sem,
+        device_id={"head": head}, device_id_type=MESH,
+    )
+
+
+def project_kernel(
+    w_hbm, g_own, ss_in, res, out,
+    w_own, w_part, g_part, s1, own1, r1o, r1n, s2, acc, r2o, r2n,
+    ss_mid, ss_core, ss_x, ss_y,
+    sem_w, sem_ws, sem_wr, sem_gs, sem_gr, sem_1s, sem_1r, sem_2s, sem_2r, sem_ss, sem_sr,
+):
+    me = lax.axis_index("head")
+    core = lax.rem(me, 2)
+    col = lax.rem(me // 2, SIDE)
+    row = me // (2 * SIDE)
+
+    def head_at(dx, dy, dc):
+        y = lax.rem(row + dy, SIDE)
+        x = lax.rem(col + dx, SIDE)
+        c = lax.rem(core + dc, 2)
+        return (y * SIDE + x) * 2 + c
+
+    partner = head_at(0, 0, 1)
+    x_peers = [head_at(k, 0, 0) for k in (1, 2, 3)]
+    y_peers = [head_at(0, k, 0) for k in (1, 2, 3)]
+    p_side = ((x_peers[0], x_peers[2]), (y_peers[0], y_peers[2]))
+    q_side = (p_side[1], p_side[0])
+
+    barrier = pltpu.get_barrier_semaphore()
+    for peer in [partner] + x_peers + y_peers:
+        pl.semaphore_signal(barrier, inc=1, device_id={"head": peer}, device_id_type=MESH)
+
+    def w_local(i, dx, dy):
+        start = pl.multiple_of(head_at(dx, dy, 0) * 256, 256)
+        return pltpu.make_async_copy(w_hbm.at[:, pl.ds(start, 256)], w_own.at[dx, dy], sem_w.at[i])
+
+    def w_remote(i, dx, dy):
+        start = pl.multiple_of(head_at(dx, dy, 1) * 256, 256)
+        return remote(w_hbm.at[:, pl.ds(start, 256)], w_part.at[dx, dy], sem_ws.at[i], sem_wr.at[i], partner)
+
+    def g_remote(c):
+        return remote(g_own.at[c], g_part.at[c], sem_gs.at[c], sem_gr.at[c], partner)
+
+    for i, (dx, dy) in enumerate(ORDER):
+        w_local(i, dx, dy).start()
+    pl.semaphore_wait(barrier, 7)
+    g_remote(0).start()
+    for i, (dx, dy) in enumerate(ORDER):
+        w_remote(i, dx, dy).start()
+    for c in range(1, CHUNKS):
+        g_remote(c).start()
+
+    def ss_core_copy():
+        return remote(ss_in, ss_core, sem_ss.at[0], sem_sr.at[0], partner)
+
+    def ss_x_copy(k):
+        return remote(ss_mid.at[0], ss_x.at[k], sem_ss.at[1 + k], sem_sr.at[1 + k], x_peers[k])
+
+    def ss_y_copy(k):
+        return remote(ss_mid.at[1], ss_y.at[k], sem_ss.at[4 + k], sem_sr.at[4 + k], y_peers[k])
+
+    ss_core_copy().start()
+
+    def first(part, c, kind):
+        if kind == 0:
+            src, dst, way = s1.at[part, c, 1, 0], r1o.at[part, c, 0], 0
+        elif kind == 1:
+            src, dst, way = s1.at[part, c, 1, 1], r1o.at[part, c, 1], 1
+        elif kind == 2:
+            src, dst, way = s1.at[part, c, 0, 1], r1n.at[part, c, 0, 1], 0
+        elif kind == 3:
+            src, dst, way = s1.at[part, c, 2, 0], r1n.at[part, c, 1, 0], 1
+        elif kind == 4:
+            src, dst, way = s1.at[part, c, 0, 0], r1n.at[part, c, 0, 0], 0
+        else:
+            src, dst, way = s1.at[part, c, 2, 1], r1n.at[part, c, 1, 1], 1
+        return remote(src, dst, sem_1s.at[part, c, kind], sem_1r.at[part, c, kind], p_side[part][way])
+
+    def second(part, c, kind):
+        if kind == 0:
+            src, dst, way = s2.at[part, c, 1, 0], r2o.at[part, c, 0], 0
+        elif kind == 1:
+            src, dst, way = s2.at[part, c, 1, 1], r2o.at[part, c, 1], 1
+        elif kind == 2:
+            src, dst, way = s2.at[part, c, 0, 1], r2n.at[part, c, 0, 1], 0
+        elif kind == 3:
+            src, dst, way = s2.at[part, c, 2, 0], r2n.at[part, c, 1, 0], 1
+        elif kind == 4:
+            src, dst, way = s2.at[part, c, 0, 0], r2n.at[part, c, 0, 0], 0
+        else:
+            src, dst, way = s2.at[part, c, 2, 1], r2n.at[part, c, 1, 1], 1
+        return remote(src, dst, sem_2s.at[part, c, kind], sem_2r.at[part, c, kind], q_side[part][way])
+
+    IMMEDIATE = {(2, 0): 0, (2, 1): 1, (1, 1): 2, (3, 0): 3}
+
+    def stage_project(c):
+        g_remote(c).wait_recv()
+        done = set()
+        for i, (dx, dy) in enumerate(ORDER):
+            @pl.when(c == 0)
+            def _():
+                w_local(i, dx, dy).wait()
+                w_remote(i, dx, dy).wait_recv()
+            term = jnp.dot(g_own[c], w_own[dx, dy], preferred_element_type=F32)
+            term += jnp.dot(g_part[c], w_part[dx, dy], preferred_element_type=F32)
+            for part, dp, dq in ((0, dx, dy), (1, dy, dx)):
+                piece = term[part * SPAN:(part + 1) * SPAN]
+                columns = pl.ds((dq % 2) * 256, 256)
+                if dp == 0:
+                    own1[part, c, dq // 2, :, columns] = piece
+                else:
+                    s1[part, c, dp - 1, dq // 2, :, columns] = piece.astype(BF16)
+                done.add((part, dp, dq))
+                pair = (part, dp, dq - dq % 2), (part, dp, dq - dq % 2 + 1)
+                kind = IMMEDIATE.get((dp, dq // 2))
+                if kind is not None and pair[0] in done and pair[1] in done:
+                    first(part, c, kind).start()
+
+    def stage_pass1(c):
+        for part in (0, 1):
+            for way, (dp, half) in enumerate(((0, 0), (2, 1))):
+                first(part, c, way).wait_recv()
+                total = s1[part, c, dp, half].astype(F32) + r1o[part, c, way].astype(F32)
+                s1[part, c, dp, half] = total.astype(BF16)
+                first(part, c, 4 + way).start()
+
+    def stage_turn(c):
+        for part in (0, 1):
+            sums = [None, None]
+            for half in (1, 0):
+                first(part, c, 2 if half else 4).wait_recv()
+                first(part, c, 5 if half else 3).wait_recv()
+                sums[half] = own1[part, c, half] + r1n[part, c, 0, half].astype(F32) + r1n[part, c, 1, half].astype(F32)
+                if half:
+                    s2[part, c, 1, 0] = sums[1][:64, :256].astype(BF16)
+                    second(part, c, 0).start()
+                    s2[part, c, 1, 1] = sums[1][64:, :256].astype(BF16)
+                    second(part, c, 1).start()
+                    s2[part, c, 2, 0] = sums[1][:64, 256:].astype(BF16)
+                    second(part, c, 3).start()
+                    s2[part, c, 2, 1] = sums[1][64:, 256:].astype(BF16)
+                else:
+                    s2[part, c, 0, 1] = sums[0][64:, 256:].astype(BF16)
+                    second(part, c, 2).start()
+                    s2[part, c, 0, 0] = sums[0][:64, 256:].astype(BF16)
+                    acc[part, c] = sums[0][:, :256]
+
+    def stage_pass2(c):
+        for part in (0, 1):
+            for way, (dp, half) in enumerate(((0, 0), (2, 1))):
+                second(part, c, way).wait_recv()
+                total = s2[part, c, dp, half].astype(F32) + r2o[part, c, way].astype(F32)
+                s2[part, c, dp, half] = total.astype(BF16)
+                second(part, c, 4 + way).start()
+
+    def stage_last(c):
+        for part in (0, 1):
+            for half in (0, 1):
+                second(part, c, 2 if half else 4).wait_recv()
+                second(part, c, 5 if half else 3).wait_recv()
+                acc[part, c, pl.ds(half * 64, 64)] += (
+                    r2n[part, c, 0, half].astype(F32) + r2n[part, c, 1, half].astype(F32)
+                )
+
+    def step(t, _):
+        @pl.when(t < CHUNKS)
+        def _():
+            stage_project(t)
+
+        @pl.when(t == 0)
+        def _():
+            ss_core_copy().wait()
+            ss_mid[0] = ss_in[...] + ss_core[...]
+            for k in range(3):
+                ss_x_copy(k).start()
+
+        @pl.when(t == 1)
+        def _():
+            for k in range(3):
+                ss_x_copy(k).wait()
+            ss_mid[1] = ss_mid[0] + ss_x[0] + ss_x[1] + ss_x[2]
+            for k in range(3):
+                ss_y_copy(k).start()
+
+        for lag, stage in ((1, stage_pass1), (2, stage_turn), (3, stage_pass2), (4, stage_last)):
+            @pl.when(jnp.logical_and(t >= lag, t < CHUNKS + lag))
+            def _():
+                stage(t - lag)
+        return 0
+
+    lax.fori_loop(0, CHUNKS + 4, step, 0)
+
+    for k in range(3):
+        ss_y_copy(k).wait()
+    total = ss_mid[1] + ss_y[0] + ss_y[1] + ss_y[2]
+    scale = lax.rsqrt(total / 16384.0 + 1e-05)
+    scale = jnp.transpose(jnp.concatenate([scale] * 16, axis=0))
+    for part in (0, 1):
+        for c in range(CHUNKS):
+            block = part * CHUNKS + c
+            rows = pl.ds(block * SPAN, SPAN)
+            out[rows, :] = (
+                res[rows, :].astype(F32) + acc[part, c] * scale[:, block:block + 1]
+            ).astype(BF16)
+
+    def drain(c, _):
+        for part in (0, 1):
+            for kind in range(6):
+                first(part, c, kind).wait_send()
+                second(part, c, kind).wait_send()
+        g_remote(c).wait_send()
+        return 0
+
+    lax.fori_loop(0, CHUNKS, drain, 0)
+    for i, (dx, dy) in enumerate(ORDER):
+        w_remote(i, dx, dy).wait_send()
+
+
+def project(w, g, ss, res):
+    vmem = pl.BlockSpec(memory_space=pltpu.VMEM)
+    dma = pltpu.SemaphoreType.DMA
+    return pl.pallas_call(
+        project_kernel,
+        out_shape=jax.ShapeDtypeStruct(res.shape, res.dtype),
+        in_specs=[pl.BlockSpec(memory_space=pl.ANY), vmem, vmem, vmem],
+        out_specs=vmem,
+        scratch_shapes=[
+            pltpu.VMEM((4, 4, 512, 256), BF16),
+            pltpu.VMEM((4, 4, 512, 256), BF16),
+            pltpu.VMEM((4, 256, 512), BF16),
+            pltpu.VMEM((2, 4, 3, 2, 128, 512), BF16),
+            pltpu.VMEM((2, 4, 2, 128, 512), F32),
+            pltpu.VMEM((2, 4, 2, 128, 512), BF16),
+            pltpu.VMEM((2, 4, 2, 2, 128, 512), BF16),
+            pltpu.VMEM((2, 4, 3, 2, 64, 256), BF16),
+            pltpu.VMEM((2, 4, 128, 256), F32),
+            pltpu.VMEM((2, 4, 2, 64, 256), BF16),
+            pltpu.VMEM((2, 4, 2, 2, 64, 256), BF16),
+            pltpu.VMEM((2, 8, 128), F32),
+            pltpu.VMEM((8, 128), F32),
+            pltpu.VMEM((3, 8, 128), F32),
+            pltpu.VMEM((3, 8, 128), F32),
+            dma((16,)), dma((16,)), dma((16,)), dma((4,)), dma((4,)),
+            dma((2, 4, 6)), dma((2, 4, 6)), dma((2, 4, 6)), dma((2, 4, 6)),
+            dma((7,)), dma((7,)),
+        ],
+        compiler_params=pltpu.CompilerParams(
+            collective_id=0, has_side_effects=True, vmem_limit_bytes=50 * 1024 * 1024
+        ),
+        cost_estimate=pl.CostEstimate(flops=8600000000, bytes_accessed=12000000, transcendentals=0),
+        name="project",
+    )(w, g, ss, res)
 
 
 def per_device(
@@ -90,17 +356,10 @@
     carried_final, outputs = lax.scan(span_step, start_state, scanned)
     outputs = jnp.moveaxis(outputs, 0, 1).reshape(row_count, head_count * head_width)
     gated = outputs * jax.nn.silu(gate_input.astype(jnp.float32))
-    squares = jnp.sum(gated * gated, axis=1)
-    totals = lax.psum(squares, "head")
-    inner_width = head_count * head_width * lax.axis_size("head")
-    scaling = lax.rsqrt(totals / inner_width + 1e-05)
-    normed = (gated * scaling[:, None] * norm_gain).astype(jnp.bfloat16)
-    partial_out = jnp.dot(normed, out_weight, preferred_element_type=jnp.float32)
-    term = lax.optimization_barrier(partial_out.astype(jnp.bfloat16)).astype(jnp.float32)
-    summed = lax.psum_scatter(
-        term.astype(jnp.bfloat16), "head", scatter_dimension=1, tiled=True
-    ).astype(jnp.float32)
-    mixed = (residual.astype(jnp.float32) + summed).astype(jnp.bfloat16)
+    ss = jnp.sum(gated * gated, axis=1).reshape(8, 128)
+    scaled_out = (gated * norm_gain).astype(jnp.bfloat16)
+    scaled_out = jnp.moveaxis(scaled_out.reshape(2, 4, 128, 512), 0, 1).reshape(4, 256, 512)
+    mixed = project(out_weight, scaled_out, ss, residual)
     return (mixed, carried_final)
 
 

time: 356 us -> 226 us (0.63)
  waiting for transfers between devices: 192 us -> 76.7 us
  blocking collectives: 62.7 us -> 0 us
  Pallas kernels: 0 us -> 59.8 us
  matrix products: 34.1 us -> 22.1 us
    reduce_scatter x1 -> x0, waiting for transfers between devices: 114 us -> none  [per_device(): lax.psum_scatter(term.astype(jnp.bfloat16), 'head', scatter_dimension=1,...]
    psum x1 -> x0, blocking collectives: 62.7 us -> none  [per_device(): totals = lax.psum(squares, 'head')]
    pallas_call x0 -> x1, Pallas kernels: none -> 59.8 us  [project(): pl.pallas_call(project_kernel, out_shape=jax.ShapeDtypeStruct(res.shape,...]
    dot_general x1 -> x0, matrix products: 16.1 us -> none  [per_device(): jnp.dot(normed, out_weight, preferred_element_type=jnp.float32)]
    dot_general x4, matrix products: 5.77 us -> 9.41 us  [span_step(): jnp.einsum('stn,shpn->sthp', reads_c.astype(jnp.float32), carried, precis...]
    unnamed x34 -> x33, local copies, waits for them, and re-layouts: 18.4 us -> 20 us
  transfers between devices with their start and end apart: 2 -> 1, of which waited for: 2 -> 1; matrix products, arithmetic and copies ran while one was open for 3% -> 5% of each run, Pallas kernels for 0% -> 0%
where the time goes in v1:
time: 226 us
  waiting for transfers between devices  76.7 us (34%)
  Pallas kernels  59.8 us (26%)
  local copies, waits for them, and re-layouts  47.3 us (21%)
  matrix products  22.1 us (10%)
  between operations  14.3 us (6%)
  other arithmetic  4.76 us (2%)
    all_gather x1, waiting for transfers between devices, per_device(): every_cache = lax.all_gather(state_cache, 'group', axis=0, tiled=True)  76 us
    pallas_call x1, Pallas kernels, project(): pl.pallas_call(project_kernel, out_shape=jax.ShapeDtypeStruct(res.shape,...  59.8 us
    unnamed x33, local copies, waits for them, and re-layouts  20 us
    dot_general x4, matrix products, span_step(): jnp.einsum('stn,shpn->sthp', reads_c.astype(jnp.float32), carried, precis...  9.41 us
    dot_general x4, matrix products, span_step(): jnp.einsum('suhp,sun->shpn', scaled, inputs_c, preferred_element_type=jnp...  5.85 us
    gather x1, local copies, waits for them, and re-layouts, per_device(): fetched = jnp.take(flat_cache, wanted, axis=0)  5.8 us
    dot_general x4, matrix products, span_step(): jnp.einsum('stn,sun->stu', reads_c, inputs_c, preferred_element_type=jnp....  4.68 us
    transpose x1, local copies, waits for them, and re-layouts, per_device(): jnp.moveaxis(outputs, 0, 1).reshape(row_count, head_count * head_width)  4.66 us
  transfers between devices with their start and end apart: 1, of which 1 were waited for; matrix products, arithmetic and copies ran while one was open for 5% of the time, Pallas kernels for 0%

profile of v1, /device:TPU:1, one launch (start us, length us, event | category | flops | bytes accessed | tf_op | source)
XLA Modules:
  0.0 225.7 jit_solution(5548855859175249515)
XLA Ops:
  10.7 3.8 %fusion.45 = (bf16[1,1024,8,256]{3,2,1,0:T(8,128)(2,1)S(1)}, bf16[1,1024,8,256]{3,2,1,0:T(8,128)(2,1)S(1)}) fusion(bf16[2,1024,8,256]{3,2,1,0:T(8,128)(2,1)} %param.19), kind=kLoop, calls=%fused_computation.76 | loop fusion | bytes 16777216 | tf_op jit(solution)/shard_map/slice | solution.py:329
  14.5 2.2 constant_dynamic-slice_fusion.2
  18.4 1.3 copy.59
  20.2 76.0 %all-gather.2.cloned.1.call-done = bf16[32,8,64,256]{3,2,1,0:T(8,128)(2,1)} async-done(((bf16[8,8,64,256]{3,2,1,0:T(8,128)(2,1)}), bf16[32,8,64,256]{3,2,1,0:T(8,128)(2,1)}) %all-gather.2.cloned.1.call-update) | async-done | bytes 8388624 | tf_op jit(solution)/shard_map/all_gather | solution.py:307
  96.3 15.3 %copy.71 = bf16[32,8,64,256]{3,1,2,0:T(8,128)(2,1)} copy(bf16[32,8,64,256]{3,2,1,0:T(8,128)(2,1)} %all-gather.2.cloned.1.call-done) | data formatting | bytes 16777216
  111.6 5.8 %gather_fusion = bf16[16,16384]{1,0:T(8,128)(2,1)S(1)} fusion(bf16[256,16384]{1,0:T(8,128)(2,1)} %bitcast.111, s32[1024]{0:T(1024)S(1)} %pad_clamp_fusion), kind=kCustom, calls=%fused_computation | custom fusion | bytes 1048640 | tf_op jit(solution)/shard_map/jit(_take)/gather | solution.py:311
  117.5 28.7 %while.13 = (s32[]{:T(128)}, f32[2,8,64,256]{3,2,1,0:T(8,128)S(1)}, f32[4,2,128,8,64]{2,4,3,1,0:T(8,128)}, f32[4,2,128,8]{3,2,0,1:T(8,128)S(1)}, f32[4,2,128,8]{...) while((s32[]{:T(128)}, f32[2,8,64,256]{3,2,1,0:T(8,128)S(1)}, ...), condition=%wide.region_2.3_spmd.clone, body=%wide.region_1.2_spmd.clone.sunk | while | flops 523259904 | bytes 6795793 | solution.py:356
  118.7 1.2 fusion.67
  121.0 2.3 %fusion.68 = f32[4,2,128,8,64]{2,4,3,1,0:T(8,128)} fusion(f32[4,2,128,8,64]{2,4,3,1,0:T(8,128)} %get-tuple-element.205, s32[]{:T(128)S(6)} %copy.99, f32[2,128,8,64]{1,3,2,0:T(8,128)S(1)} %convolution_bitcast_fusion.2, f32[2,8,64,256]{3,2,1,0:T(8,128)S(1)} %get-tuple-element.204, f32[8]{0:T(128)S(1)} %get-tuple-element.221, ...), kind=kOutput, calls=%fused_computation.7.clone.1 | convolution fusion | flops 403308544 | bytes 2499616 | tf_op jit(solution)/shard_map/while/body/eval_jaxpr/stn,shpn->sthp/dot_general | solution.py:343
  123.4 1.5 convolution_add_fusion.2
  125.8 1.2 fusion.67
  128.1 2.3 %fusion.68 = f32[4,2,128,8,64]{2,4,3,1,0:T(8,128)} fusion(f32[4,2,128,8,64]{2,4,3,1,0:T(8,128)} %get-tuple-element.205, s32[]{:T(128)S(6)} %copy.99, f32[2,128,8,64]{1,3,2,0:T(8,128)S(1)} %convolution_bitcast_fusion.2, f32[2,8,64,256]{3,2,1,0:T(8,128)S(1)} %get-tuple-element.204, f32[8]{0:T(128)S(1)} %get-tuple-element.221, ...), kind=kOutput, calls=%fused_computation.7.clone.1 | convolution fusion | flops 403308544 | bytes 2499616 | tf_op jit(solution)/shard_map/while/body/eval_jaxpr/stn,shpn->sthp/dot_general | solution.py:343
  130.5 1.5 convolution_add_fusion.2
  132.9 1.2 fusion.67
  135.2 2.4 %fusion.68 = f32[4,2,128,8,64]{2,4,3,1,0:T(8,128)} fusion(f32[4,2,128,8,64]{2,4,3,1,0:T(8,128)} %get-tuple-element.205, s32[]{:T(128)S(6)} %copy.99, f32[2,128,8,64]{1,3,2,0:T(8,128)S(1)} %convolution_bitcast_fusion.2, f32[2,8,64,256]{3,2,1,0:T(8,128)S(1)} %get-tuple-element.204, f32[8]{0:T(128)S(1)} %get-tuple-element.221, ...), kind=kOutput, calls=%fused_computation.7.clone.1 | convolution fusion | flops 403308544 | bytes 2499616 | tf_op jit(solution)/shard_map/while/body/eval_jaxpr/stn,shpn->sthp/dot_general | solution.py:343
  137.6 1.5 convolution_add_fusion.2
  140.0 1.2 fusion.67
  142.3 2.4 %fusion.68 = f32[4,2,128,8,64]{2,4,3,1,0:T(8,128)} fusion(f32[4,2,128,8,64]{2,4,3,1,0:T(8,128)} %get-tuple-element.205, s32[]{:T(128)S(6)} %copy.99, f32[2,128,8,64]{1,3,2,0:T(8,128)S(1)} %convolution_bitcast_fusion.2, f32[2,8,64,256]{3,2,1,0:T(8,128)S(1)} %get-tuple-element.204, f32[8]{0:T(128)S(1)} %get-tuple-element.221, ...), kind=kOutput, calls=%fused_computation.7.clone.1 | convolution fusion | flops 403308544 | bytes 2499616 | tf_op jit(solution)/shard_map/while/body/eval_jaxpr/stn,shpn->sthp/dot_general | solution.py:343
  144.7 1.5 convolution_add_fusion.2
  146.2 4.7 %copy.58 = f32[2,4,128,8,64]{2,1,0,4,3:T(4,128)} copy(f32[2,4,128,8,64]{2,4,3,0,1:T(8,128)} %bitcast.118) | data formatting | bytes 4194304 | tf_op jit(solution)/shard_map/transpose | solution.py:357
  150.9 3.2 %reshape.185 = f32[1024,512]{0,1:T(8,128)} reshape(f32[2,4,128,8,64]{2,1,0,4,3:T(4,128)} %copy.58) | data formatting | bytes 4194304 | tf_op jit(solution)/shard_map/reshape | solution.py:357
  154.1 2.4 %multiply_reduce_fusion = (f32[1024]{0:T(1024)S(1)}, bf16[1024,512]{0,1:T(8,128)(2,1)S(1)}) fusion(f32[1024,512]{0,1:T(8,128)} %reshape.185, bf16[1024,512]{0,1:T(8,128)(2,1)S(1)} %copy-done.2, f32[512]{0:T(512)S(1)} %copy-done.9), kind=kLoop, calls=%fused_computation.52 | loop fusion | flops 5241856 | bytes 4200448 | tf_op jit(solution)/shard_map/reduce_sum | solution.py:359
  157.2 1.0 copy.60
  158.2 59.8 %project.1 = bf16[1024,256]{1,0:T(8,128)(2,1)S(1)} custom-call(bf16[512,8192]{1,0:T(8,128)(2,1)} %w_hbm.1, bf16[4,256,512]{2,1,0:T(8,128)(2,1)S(1)} %bitcast.108, f32[8,128]{1,0:T(8,128)S(1)} %bitcast.109, bf16[1024,256]{1,0:T(8,128)(2,1)S(1)} %copy-done), custom_call_target="tpu_custom_call" | custom-call | flops 8600000512 | bytes 12000000 | tf_op jit(solution)/shard_map/project/pallas_call | solution.py:242
  (116 shorter events, 15.5 us)
Async XLA Ops:
  7.2 0.8 copy-start.10
  7.2 0.8 copy-start.11
  7.2 0.9 copy-start.13
  7.2 0.9 copy-start.14
  7.2 1.0 copy-start.7
  7.2 1.0 copy-start.12
  7.2 1.9 copy-start.5
  7.2 89.1 %all-gather.2.cloned.1.call-start = ((), (), s32[]{:S(2)}) async-start(), calls=%async_computation | async-start | bytes 10485760 | tf_op jit(solution)/shard_map/all_gather | solution.py:307
  16.7 1.8 copy-start.6
  111.5 6.0 %copy-start.8 = (f32[8]{0:T(128)S(1)}, f32[8]{0:T(128)}, u32[]{:S(2)}) copy-start(f32[8]{0:T(128)} %param.22) | copy-start | bytes 100
  117.8 2.4 %copy-start.3 = (f32[4,2,128,8]{3,2,0,1:T(8,128)}, f32[4,2,128,8]{3,2,0,1:T(8,128)S(1)}, u32[]{:S(2)}) copy-start(f32[4,2,128,8]{3,2,0,1:T(8,128)S(1)} %get-tuple-element.216) | copy-start | bytes 98308 | tf_op jit(solution)/shard_map/while
  123.3 1.5 copy-start.4
  124.9 2.4 %copy-start.3 = (f32[4,2,128,8]{3,2,0,1:T(8,128)}, f32[4,2,128,8]{3,2,0,1:T(8,128)S(1)}, u32[]{:S(2)}) copy-start(f32[4,2,128,8]{3,2,0,1:T(8,128)S(1)} %get-tuple-element.216) | copy-start | bytes 98308 | tf_op jit(solution)/shard_map/while
  130.4 1.5 copy-start.4
  132.0 2.4 %copy-start.3 = (f32[4,2,128,8]{3,2,0,1:T(8,128)}, f32[4,2,128,8]{3,2,0,1:T(8,128)S(1)}, u32[]{:S(2)}) copy-start(f32[4,2,128,8]{3,2,0,1:T(8,128)S(1)} %get-tuple-element.216) | copy-start | bytes 98308 | tf_op jit(solution)/shard_map/while
  137.5 1.5 copy-start.4
  139.1 2.4 %copy-start.3 = (f32[4,2,128,8]{3,2,0,1:T(8,128)}, f32[4,2,128,8]{3,2,0,1:T(8,128)S(1)}, u32[]{:S(2)}) copy-start(f32[4,2,128,8]{3,2,0,1:T(8,128)S(1)} %get-tuple-element.216) | copy-start | bytes 98308 | tf_op jit(solution)/shard_map/while
  144.7 1.5 copy-start.4
  146.2 4.7 %copy-start.1 = (f32[2,8,64,256]{3,2,1,0:T(8,128)}, f32[2,8,64,256]{3,2,1,0:T(8,128)S(1)}, u32[]{:S(2)}) copy-start(f32[2,8,64,256]{3,2,1,0:T(8,128)S(1)} %get-tuple-element.226) | copy-start | bytes 3145732
  150.9 3.2 %copy-start.2 = (bf16[1024,512]{0,1:T(8,128)(2,1)S(1)}, bf16[1024,512]{0,1:T(8,128)(2,1)}, u32[]{:S(2)}) copy-start(bf16[1024,512]{0,1:T(8,128)(2,1)} %copy.59) | copy-start | bytes 3145732
  150.9 3.2 %copy-start.9 = (f32[512]{0:T(512)S(1)}, f32[512]{0:T(512)}, u32[]{:S(2)}) copy-start(f32[512]{0:T(512)} %param.23) | copy-start | bytes 6148
  156.4 1.8 copy-start
Sparse Core Ops, SparseCore 0:
  9.7 86.5 all-gather.1

commit v2 on v1

--- a/solution.py
+++ b/solution.py
@@ -6,30 +6,50 @@
 from jax.sharding import PartitionSpec as P
 
 SPAN = 128
-
-HALF = (0, 1)
-ORDER = ((2, 0), (2, 1), (0, 2), (1, 2), (2, 2), (2, 3), (3, 2), (1, 3), (3, 0), (3, 1), (0, 3), (1, 0), (1, 1), (3, 3), (0, 1), (0, 0))
+CAP = 6
+ORDER = (
+    (2, 0), (2, 1), (0, 2), (1, 2), (2, 2), (2, 3), (3, 2), (1, 3),
+    (3, 0), (3, 1), (0, 3), (1, 0), (1, 1), (3, 3), (0, 1), (0, 0),
+)
 SIDE = 4
 CHUNKS = 4
+BLOCKS = 8
 MESH = pl.DeviceIdType.MESH
 BF16 = jnp.bfloat16
 F32 = jnp.float32
-
-
-def remote(src, dst, send_sem, recv_sem, head):
+I32 = jnp.int32
+HIGHEST = lax.Precision.HIGHEST
+
+
+def remote(src, dst, send_sem, recv_sem, where):
     return pltpu.make_async_remote_copy(
         src_ref=src, dst_ref=dst, send_sem=send_sem, recv_sem=recv_sem,
-        device_id={"head": head}, device_id_type=MESH,
+        device_id=where, device_id_type=MESH,
     )
 
 
-def project_kernel(
-    w_hbm, g_own, ss_in, res, out,
-    w_own, w_part, g_part, s1, own1, r1o, r1n, s2, acc, r2o, r2n,
+def dot_tn(a, b):
+    return lax.dot_general(a, b, (((0,), (0,)), ((), ())), preferred_element_type=F32)
+
+
+def dot_nt(a, b):
+    return lax.dot_general(a, b, (((1,), (1,)), ((), ())), preferred_element_type=F32)
+
+
+def mixer_kernel(
+    owner_s, slot_s, spans_s, decay_s, bias_s, skip_s,
+    x_hbm, gate_hbm, step_hbm, sp_hbm, gain_hbm, w_hbm, res_hbm, cache_hbm,
+    out, state_out,
+    x_v, gate_v, step_v, sp_v, gain_v, res, cache_v,
+    req_v, rreq, req_s, idx_s, pbuf, rbuf, relay,
+    e_v, f_v, em_v, sel_v, yi_v, ee_v, u_v, c_v, h_v, hb_v, ssa, ss_in,
+    w_own, w_part, g_own, g_part, s1, own1, r1o, r1n, s2, acc, r2o, r2n,
     ss_mid, ss_core, ss_x, ss_y,
+    sem_in, sem_sp, sem_req_s, sem_req_r, sem_rs, sem_st_s, sem_st_r, sem_out,
     sem_w, sem_ws, sem_wr, sem_gs, sem_gr, sem_1s, sem_1r, sem_2s, sem_2r, sem_ss, sem_sr,
 ):
     me = lax.axis_index("head")
+    deep = lax.axis_index("group")
     core = lax.rem(me, 2)
     col = lax.rem(me // 2, SIDE)
     row = me // (2 * SIDE)
@@ -40,15 +60,31 @@
         c = lax.rem(core + dc, 2)
         return (y * SIDE + x) * 2 + c
 
-    partner = head_at(0, 0, 1)
-    x_peers = [head_at(k, 0, 0) for k in (1, 2, 3)]
-    y_peers = [head_at(0, k, 0) for k in (1, 2, 3)]
+    def at_head(h):
+        return {"head": h}
+
+    partner = at_head(head_at(0, 0, 1))
+    x_peers = [at_head(head_at(k, 0, 0)) for k in (1, 2, 3)]
+    y_peers = [at_head(head_at(0, k, 0)) for k in (1, 2, 3)]
+    z_peers = [{"group": lax.rem(deep + k, 4)} for k in (1, 2, 3)]
     p_side = ((x_peers[0], x_peers[2]), (y_peers[0], y_peers[2]))
     q_side = (p_side[1], p_side[0])
 
     barrier = pltpu.get_barrier_semaphore()
-    for peer in [partner] + x_peers + y_peers:
-        pl.semaphore_signal(barrier, inc=1, device_id={"head": peer}, device_id_type=MESH)
+    for peer in z_peers + [partner] + x_peers + y_peers:
+        pl.semaphore_signal(barrier, inc=1, device_id=peer, device_id_type=MESH)
+
+    loads = [
+        pltpu.make_async_copy(src, dst, sem_in.at[i])
+        for i, (src, dst) in enumerate((
+            (cache_hbm, cache_v), (step_hbm, step_v), (x_hbm, x_v), (gain_hbm, gain_v),
+            (gate_hbm, gate_v), (res_hbm, res),
+        ))
+    ]
+
+    def sp_copy(b):
+        start = pl.multiple_of(b * 1024, 1024)
+        return pltpu.make_async_copy(sp_hbm.at[:, pl.ds(start, 1024)], sp_v.at[b], sem_sp.at[b])
 
     def w_local(i, dx, dy):
         start = pl.multiple_of(head_at(dx, dy, 0) * 256, 256)
@@ -61,14 +97,162 @@
     def g_remote(c):
         return remote(g_own.at[c], g_part.at[c], sem_gs.at[c], sem_gr.at[c], partner)
 
+    for load in loads[:5]:
+        load.start()
+    for b in range(BLOCKS):
+        sp_copy(b).start()
+
+    lane = lax.broadcasted_iota(I32, (8, 128), 1)
+    request = jnp.zeros((8, 128), I32)
+    seen = jnp.zeros((8, 128), I32)
+    counts = [jnp.int32(0)] * 4
+    for e in range(16):
+        s, j = divmod(e, 8)
+        owner = owner_s[s, j]
+        place = slot_s[s, j] * 8 + j
+        named = (lane // 8) == owner
+        request = jnp.where(jnp.logical_and(named, seen == lane % 8), place, request)
+        seen = seen + jnp.where(named, 1, 0)
+        rank = jnp.int32(0)
+        for q in range(4):
+            rank = jnp.where(owner == q, counts[q], rank)
+            counts[q] = counts[q] + jnp.where(owner == q, 1, 0)
+        away = lax.rem(owner - deep + 4, 4)
+        idx_s[0, e] = jnp.where(away == 0, 0, (away - 1) * CAP + jnp.minimum(rank, CAP - 1))
+        idx_s[1, e] = jnp.where(away == 0, 1, 0)
+        idx_s[2, e] = place
+    req_v[...] = request
+
+    def req_copy(k):
+        return remote(req_v, rreq.at[k], sem_req_s.at[k], sem_req_r.at[k], z_peers[k])
+
+    pl.semaphore_wait(barrier, 10)
+    for k in (1, 0, 2):
+        req_copy(k).start()
     for i, (dx, dy) in enumerate(ORDER):
         w_local(i, dx, dy).start()
-    pl.semaphore_wait(barrier, 7)
-    g_remote(0).start()
     for i, (dx, dy) in enumerate(ORDER):
         w_remote(i, dx, dy).start()
-    for c in range(1, CHUNKS):
+    loads[5].start()
+
+    sub = lax.broadcasted_iota(I32, (8, 128), 0)
+    bias = jnp.zeros((8, 128), F32)
+    decay = jnp.zeros((8, 128), F32)
+    for j in range(8):
+        bias = jnp.where(sub == j, bias_s[j], bias)
+        decay = jnp.where(sub == j, decay_s[j], decay)
+    decay = -jnp.exp(decay)
+    loads[1].wait()
+    steps = []
+    for b in range(BLOCKS):
+        raw = step_v[:, b * SPAN:(b + 1) * SPAN] + bias
+        alive = jnp.where(b % CHUNKS < spans_s[b // CHUNKS], 1.0, 0.0)
+        steps.append((jnp.maximum(raw, 0.0) + jnp.log1p(jnp.exp(-jnp.abs(raw)))) * alive)
+    dt = jnp.concatenate(steps, axis=0)
+    rate = jnp.concatenate([decay * step for step in steps], axis=0)
+    square0 = lax.broadcasted_iota(I32, (SPAN, SPAN), 0)
+    square1 = lax.broadcasted_iota(I32, (SPAN, SPAN), 1)
+    upper = jnp.where(square0 <= square1, 1.0, 0.0).astype(F32)
+    cum = jnp.dot(rate, upper, precision=HIGHEST, preferred_element_type=F32)
+    middle = cum[:, SPAN - 1:] * 0.5
+    e_v[...] = jnp.exp(cum - middle)
+    f_v[...] = jnp.exp(middle - cum) * dt
+    em_v[...] = jnp.exp(jnp.broadcast_to(middle, (BLOCKS * 8, 128)))
+    ssa[...] = jnp.zeros((SPAN, SPAN), F32)
+
+    def rank_copy(k):
+        return pltpu.make_async_copy(rreq.at[k], req_s.at[k], sem_rs.at[k])
+
+    def state_copy(i):
+        src, dst, way = (
+            (pbuf.at[pl.ds(6, 3)], relay.at[0], 0),
+            (pbuf.at[pl.ds(9, 3)], relay.at[1], 2),
+            (pbuf.at[pl.ds(0, 6)], rbuf.at[pl.ds(0, 6)], 2),
+            (pbuf.at[pl.ds(12, 6)], rbuf.at[pl.ds(12, 6)], 0),
+            (relay.at[0], rbuf.at[pl.ds(6, 3)], 0),
+            (relay.at[1], rbuf.at[pl.ds(9, 3)], 2),
+        )[i]
+        return remote(src, dst, sem_st_s.at[i], sem_st_r.at[i], z_peers[way])
+
+    loads[0].wait()
+    for k in (1, 0, 2):
+        req_copy(k).wait_recv()
+        rank_copy(k).start()
+    for k in (1, 0, 2):
+        rank_copy(k).wait()
+        for r in range(CAP):
+            pbuf[k * CAP + r] = cache_v[req_s[k, 0, deep * 8 + r]]
+            if k == 1 and r == 2:
+                state_copy(0).start()
+        state_copy((2, 1, 3)[k]).start()
+
+    pick = me // 4
+    sel_v[...] = jnp.where(
+        lax.broadcasted_iota(I32, (SPAN, 1024), 1) == lax.broadcasted_iota(I32, (SPAN, 1024), 0) * 8 + pick, 1.0, 0.0
+    ).astype(BF16)
+    channel = lax.broadcasted_iota(I32, (16, 512), 1)
+    spread = jnp.where(channel // 64 == lax.broadcasted_iota(I32, (16, 512), 0) % 8, 1.0, 0.0).astype(BF16)
+    channel = lax.broadcasted_iota(I32, (1, 512), 1)
+    skip = jnp.zeros((1, 512), F32)
+    for j in range(8):
+        skip = jnp.where(channel // 64 == j, skip_s[j], skip)
+    for load in loads[2:5]:
+        load.wait()
+
+    def widen(part):
+        high = part.astype(BF16)
+        low = (part - high.astype(F32)).astype(BF16)
+        return dot_tn(jnp.concatenate([high, low], axis=0), spread)
+
+    def prepare(b, _):
+        sp_copy(b).wait()
+        few = pl.ds(pl.multiple_of(b * 8, 8), 8)
+        x = x_v[pl.ds(pl.multiple_of(b * SPAN, SPAN), SPAN), :].astype(F32)
+        wide_e = widen(e_v[few, :])
+        ee_v[b] = wide_e
+        z = (widen(f_v[few, :]) * x).astype(BF16)
+        b_rows = jnp.dot(sel_v[...], sp_v[b, 0], preferred_element_type=F32).astype(BF16)
+        c_rows = jnp.dot(sel_v[...], sp_v[b, 1], preferred_element_type=F32).astype(BF16)
+        c_v[b] = c_rows
+        scores = jnp.where(square0 >= square1, dot_nt(c_rows, b_rows), 0.0).astype(BF16)
+        yi_v[b] = wide_e * jnp.dot(scores, z, preferred_element_type=F32) + skip * x
+        u_v[b] = dot_tn(z, b_rows)
+
+        @pl.when(b == 2)
+        def _():
+            for i in (0, 1):
+                state_copy(i).wait_recv()
+                state_copy(4 + i).start()
+        return 0
+
+    lax.fori_loop(0, BLOCKS, prepare, 0)
+
+    for i in (2, 3, 4, 5):
+        state_copy(i).wait_recv()
+    for e in range(16):
+        s, j = divmod(e, 8)
+        here = cache_v[idx_s[2, e]].astype(F32)
+        sent = rbuf[idx_s[0, e]].astype(F32)
+        h_v[s, j * 64:(j + 1) * 64, :] = jnp.where(idx_s[1, e] == 1, here, sent)
+
+    def stage_states(c):
+        for s in (0, 1):
+            b = s * CHUNKS + c
+            for j in range(8):
+                rows = slice(j * 64, (j + 1) * 64)
+                fade = em_v[pl.ds(b * 8 + j, 1), :]
+                fade = jnp.concatenate([fade, fade], axis=1)
+                faded = h_v[s, rows, :] * fade
+                hb_v[s, rows, :] = faded.astype(BF16)
+                h_v[s, rows, :] = (faded + u_v[b, rows, :]) * fade
+            y = yi_v[b] + ee_v[b] * dot_nt(c_v[b], hb_v[s])
+            gate = gate_v[pl.ds(pl.multiple_of(b * SPAN, SPAN), SPAN), :].astype(F32)
+            gated = y * (gate / (1.0 + jnp.exp(-gate)))
+            ssa[...] = jnp.where(square1 == b, jnp.sum(gated * gated, axis=1, keepdims=True), ssa[...])
+            g_own[c, s * SPAN:(s + 1) * SPAN, :] = (gated * gain_v[...]).astype(BF16)
         g_remote(c).start()
+
+    final_copy = pltpu.make_async_copy(h_v, state_out, sem_out)
 
     def ss_core_copy():
         return remote(ss_in, ss_core, sem_ss.at[0], sem_sr.at[0], partner)
@@ -78,8 +262,6 @@
 
     def ss_y_copy(k):
         return remote(ss_mid.at[1], ss_y.at[k], sem_ss.at[4 + k], sem_sr.at[4 + k], y_peers[k])
-
-    ss_core_copy().start()
 
     def first(part, c, kind):
         if kind == 0:
@@ -183,18 +365,28 @@
                 )
 
     def step(t, _):
+        @pl.when(t < CHUNKS - 1)
+        def _():
+            stage_states(t + 1)
+
         @pl.when(t < CHUNKS)
         def _():
             stage_project(t)
 
-        @pl.when(t == 0)
+        @pl.when(t == 2)
+        def _():
+            final_copy.start()
+            ss_in[...] = jnp.transpose(ssa[...])[:8]
+            ss_core_copy().start()
+
+        @pl.when(t == 3)
         def _():
             ss_core_copy().wait()
             ss_mid[0] = ss_in[...] + ss_core[...]
             for k in range(3):
                 ss_x_copy(k).start()
 
-        @pl.when(t == 1)
+        @pl.when(t == 4)
         def _():
             for k in range(3):
                 ss_x_copy(k).wait()
@@ -208,7 +400,9 @@
                 stage(t - lag)
         return 0
 
+    stage_states(0)
     lax.fori_loop(0, CHUNKS + 4, step, 0)
+    loads[5].wait()
 
     for k in range(3):
         ss_y_copy(k).wait()
@@ -234,19 +428,56 @@
     lax.fori_loop(0, CHUNKS, drain, 0)
     for i, (dx, dy) in enumerate(ORDER):
         w_remote(i, dx, dy).wait_send()
-
-
-def project(w, g, ss, res):
+    for k in range(3):
+        req_copy(k).wait_send()
+    for i in range(6):
+        state_copy(i).wait_send()
+    final_copy.wait()
+
+
+def mixer(owner, slot, spans, decay, bias, skip, x, gate, step, sp, gain, w, res, cache):
     vmem = pl.BlockSpec(memory_space=pltpu.VMEM)
+    smem = pl.BlockSpec(memory_space=pltpu.SMEM)
+    hbm = pl.BlockSpec(memory_space=pl.ANY)
     dma = pltpu.SemaphoreType.DMA
     return pl.pallas_call(
-        project_kernel,
-        out_shape=jax.ShapeDtypeStruct(res.shape, res.dtype),
-        in_specs=[pl.BlockSpec(memory_space=pl.ANY), vmem, vmem, vmem],
-        out_specs=vmem,
+        mixer_kernel,
+        out_shape=(
+            jax.ShapeDtypeStruct(res.shape, res.dtype),
+            jax.ShapeDtypeStruct((2, 512, 256), F32),
+        ),
+        in_specs=[smem] * 6 + [hbm] * 8,
+        out_specs=(vmem, hbm),
         scratch_shapes=[
+            pltpu.VMEM((1024, 512), BF16),
+            pltpu.VMEM((1024, 512), BF16),
+            pltpu.VMEM((8, 1024), F32),
+            pltpu.VMEM((8, 2, 1024, 256), BF16),
+            pltpu.VMEM((1, 512), F32),
+            pltpu.VMEM((1024, 256), BF16),
+            pltpu.VMEM((64, 64, 256), BF16),
+            pltpu.VMEM((8, 128), I32),
+            pltpu.VMEM((3, 8, 128), I32),
+            pltpu.SMEM((3, 8, 128), I32),
+            pltpu.SMEM((3, 16), I32),
+            pltpu.VMEM((18, 64, 256), BF16),
+            pltpu.VMEM((18, 64, 256), BF16),
+            pltpu.VMEM((2, 3, 64, 256), BF16),
+            pltpu.VMEM((64, 128), F32),
+            pltpu.VMEM((64, 128), F32),
+            pltpu.VMEM((64, 128), F32),
+            pltpu.VMEM((128, 1024), BF16),
+            pltpu.VMEM((8, 128, 512), F32),
+            pltpu.VMEM((8, 128, 512), F32),
+            pltpu.VMEM((8, 512, 256), F32),
+            pltpu.VMEM((8, 128, 256), BF16),
+            pltpu.VMEM((2, 512, 256), F32),
+            pltpu.VMEM((2, 512, 256), BF16),
+            pltpu.VMEM((128, 128), F32),
+            pltpu.VMEM((8, 128), F32),
             pltpu.VMEM((4, 4, 512, 256), BF16),
             pltpu.VMEM((4, 4, 512, 256), BF16),
+            pltpu.VMEM((4, 256, 512), BF16),
             pltpu.VMEM((4, 256, 512), BF16),
             pltpu.VMEM((2, 4, 3, 2, 128, 512), BF16),
             pltpu.VMEM((2, 4, 2, 128, 512), F32),
@@ -260,107 +491,29 @@
             pltpu.VMEM((8, 128), F32),
             pltpu.VMEM((3, 8, 128), F32),
             pltpu.VMEM((3, 8, 128), F32),
+            dma((6,)), dma((8,)), dma((3,)), dma((3,)), dma((3,)), dma((6,)), dma((6,)), dma(()),
             dma((16,)), dma((16,)), dma((16,)), dma((4,)), dma((4,)),
             dma((2, 4, 6)), dma((2, 4, 6)), dma((2, 4, 6)), dma((2, 4, 6)),
             dma((7,)), dma((7,)),
         ],
         compiler_params=pltpu.CompilerParams(
-            collective_id=0, has_side_effects=True, vmem_limit_bytes=50 * 1024 * 1024
+            collective_id=0, has_side_effects=True, vmem_limit_bytes=62 * 1024 * 1024
         ),
-        cost_estimate=pl.CostEstimate(flops=8600000000, bytes_accessed=12000000, transcendentals=0),
-        name="project",
-    )(w, g, ss, res)
+        cost_estimate=pl.CostEstimate(flops=10000000000, bytes_accessed=24000000, transcendentals=0),
+        name="mixer",
+    )(owner, slot, spans, decay, bias, skip, x, gate, step, sp, gain, w, res, cache)
 
 
 def per_device(
-    mixer_input,
-    gate_input,
-    step_raw,
-    state_proj,
-    decay_log,
-    step_bias,
-    skip_gain,
-    norm_gain,
-    out_weight,
-    residual,
-    new_spans,
-    hit_owner,
-    hit_slot,
-    state_cache,
+    mixer_input, gate_input, step_raw, state_proj, decay_log, step_bias, skip_gain, norm_gain,
+    out_weight, residual, new_spans, hit_owner, hit_slot, state_cache,
 ):
-    highest = lax.Precision.HIGHEST
-    session_count = new_spans.shape[0]
-    head_count = decay_log.shape[0]
-    row_count = mixer_input.shape[0]
-    turn_length = row_count // session_count
-    span_count = turn_length // SPAN
-    head_width = mixer_input.shape[1] // head_count
-    state_width = state_proj.shape[3]
-    group_count = state_proj.shape[2]
-    per_group = head_count * lax.axis_size("head") // group_count
-    group_index = lax.axis_index("head") * head_count // per_group
-    block_count = session_count * head_count
-    owners = hit_owner.reshape(block_count)
-    slot_index = hit_slot.reshape(block_count)
-    local_head = jnp.arange(block_count, dtype=jnp.int32) % head_count
-    flat_width = head_width * state_width
-    every_cache = lax.all_gather(state_cache, "group", axis=0, tiled=True)
-    slot_count = state_cache.shape[0]
-    flat_cache = every_cache.reshape(-1, flat_width)
-    wanted = (owners * slot_count + slot_index) * head_count + local_head
-    fetched = jnp.take(flat_cache, wanted, axis=0)
-    start_state = fetched.astype(jnp.float32).reshape(
-        session_count, head_count, head_width, state_width
+    mixed, final = mixer(
+        hit_owner, hit_slot, new_spans, decay_log, step_bias, skip_gain,
+        mixer_input, gate_input, step_raw.T, state_proj.reshape(2, 8192, 256),
+        norm_gain.reshape(1, 512), out_weight, residual, state_cache.reshape(64, 64, 256),
     )
-    live = (jnp.arange(turn_length, dtype=jnp.int32)[None, :] < (new_spans * SPAN)[:, None]).astype(
-        jnp.float32
-    )
-    steps = (
-        jax.nn.softplus(step_raw.reshape(session_count, turn_length, head_count) + step_bias)
-        * live[:, :, None]
-    )
-    rates = -jnp.exp(decay_log) * steps
-    shape_four = (session_count, span_count, SPAN, head_count)
-    steps = steps.reshape(shape_four)
-    cumulative = jnp.cumsum(rates.reshape(shape_four), axis=2)
-    values = mixer_input.reshape(session_count, span_count, SPAN, head_count, head_width)
-    inputs_b = lax.dynamic_index_in_dim(state_proj[0], group_index, 1, keepdims=False)
-    inputs_b = inputs_b.reshape(session_count, span_count, SPAN, state_width)
-    outputs_c = lax.dynamic_index_in_dim(state_proj[1], group_index, 1, keepdims=False)
-    outputs_c = outputs_c.reshape(session_count, span_count, SPAN, state_width)
-    lower = jnp.arange(SPAN)[:, None] >= jnp.arange(SPAN)[None, :]
-
-    def span_step(carried, inputs):
-        values_c, inputs_c, reads_c, steps_c, cumul_c = inputs
-        scores = jnp.einsum("stn,sun->stu", reads_c, inputs_c, preferred_element_type=jnp.float32)
-        differ = cumul_c[:, :, None] - cumul_c[:, None, :]
-        weights = jnp.where(lower[None, :, :, None], jnp.exp(jnp.minimum(differ, 0.0)), 0.0)
-        weights = (weights * scores[..., None] * steps_c[:, None]).astype(jnp.bfloat16)
-        within = jnp.einsum(
-            "stuh,suhp->sthp", weights, values_c, preferred_element_type=jnp.float32
-        )
-        carried_in = (
-            jnp.einsum("stn,shpn->sthp", reads_c.astype(jnp.float32), carried, precision=highest)
-            * jnp.exp(cumul_c)[..., None]
-        )
-        to_end = jnp.exp(cumul_c[:, -1:] - cumul_c) * steps_c
-        scaled = (to_end[..., None] * values_c.astype(jnp.float32)).astype(jnp.bfloat16)
-        update = jnp.einsum("suhp,sun->shpn", scaled, inputs_c, preferred_element_type=jnp.float32)
-        carried_next = jnp.exp(cumul_c[:, -1])[..., None, None] * carried + update
-        result = within + carried_in + skip_gain[None, None, :, None] * values_c.astype(jnp.float32)
-        return (carried_next, result)
-
-    scanned = tuple(
-        (jnp.moveaxis(member, 1, 0) for member in (values, inputs_b, outputs_c, steps, cumulative))
-    )
-    carried_final, outputs = lax.scan(span_step, start_state, scanned)
-    outputs = jnp.moveaxis(outputs, 0, 1).reshape(row_count, head_count * head_width)
-    gated = outputs * jax.nn.silu(gate_input.astype(jnp.float32))
-    ss = jnp.sum(gated * gated, axis=1).reshape(8, 128)
-    scaled_out = (gated * norm_gain).astype(jnp.bfloat16)
-    scaled_out = jnp.moveaxis(scaled_out.reshape(2, 4, 128, 512), 0, 1).reshape(4, 256, 512)
-    mixed = project(out_weight, scaled_out, ss, residual)
-    return (mixed, carried_final)
+    return mixed, final.reshape(2, 8, 64, 256)
 
 
 def solution(mesh):

time: 226 us -> 82.5 us (0.37)
  waiting for transfers between devices: 76.7 us -> 0 us
  local copies, waits for them, and re-layouts: 47.3 us -> 4.16 us
  matrix products: 22.1 us -> 0 us
  Pallas kernels: 59.8 us -> 77.5 us
  between operations: 14.3 us -> 0.64 us
  other arithmetic: 4.76 us -> 0 us
    all_gather x1 -> x0, waiting for transfers between devices: 76 us -> none  [per_device(): every_cache = lax.all_gather(state_cache, 'group', axis=0, tiled=True)]
    dot_general x16 -> x0, matrix products: 22.1 us -> none  [the longest x4 9.41 us: span_step(): jnp.einsum('stn,shpn->sthp', reads_c.astype(jnp.float32), carried, precis...]
    pallas_call x1, Pallas kernels: 59.8 us -> 77.5 us  [mixer(): pl.pallas_call(mixer_kernel, out_shape=(jax.ShapeDtypeStruct(res.shape, r...]
    unnamed x33 -> x2, local copies, waits for them, and re-layouts: 20 us -> 4.16 us
    dynamic_slice x17 -> x0, local copies, waits for them, and re-layouts: 6.12 us -> none  [the longest x16 3.96 us: per_device(): carried_final, outputs = lax.scan(span_step, start_state, scanned)]
    gather x1 -> x0, local copies, waits for them, and re-layouts: 5.8 us -> none  [per_device(): fetched = jnp.take(flat_cache, wanted, axis=0)]
    reshape x4 -> x0, local copies, waits for them, and re-layouts: 5.65 us -> none  [the longest x1 3.16 us: per_device(): jnp.moveaxis(outputs, 0, 1).reshape(row_count, head_count * head_width)]
    transpose x1 -> x0, local copies, waits for them, and re-layouts: 4.66 us -> none  [per_device(): jnp.moveaxis(outputs, 0, 1).reshape(row_count, head_count * head_width)]
  transfers between devices with their start and end apart: 1 -> 0, of which waited for: 1 -> 0; matrix products, arithmetic and copies ran while one was open for 5% -> 0% of each run, Pallas kernels for 0% -> 0%
where the time goes in v2:
time: 82.5 us; the launch traced here: 82.3 us
  Pallas kernels  77.5 us (94%)
  local copies, waits for them, and re-layouts  4.16 us (5%)
    pallas_call x1, Pallas kernels, mixer(): pl.pallas_call(mixer_kernel, out_shape=(jax.ShapeDtypeStruct(res.shape, r...  77.5 us
    unnamed x2, local copies, waits for them, and re-layouts  4.16 us

profile of v2, /device:TPU:1, one launch (start us, length us, event | category | flops | bytes accessed | tf_op | source)
XLA Modules:
  0.0 82.3 jit_solution(9909825373523664924)
XLA Ops:
  0.6 77.5 %mixer.1 = (bf16[1024,256]{1,0:T(8,128)(2,1)}, f32[2,512,256]{2,1,0:T(8,128)}) custom-call(s32[2,8]{1,0:T(2,128)} %owner_s.1, s32[2,8]{1,0:T(2,128)} %slot_s.1, s32[2]{0:T(128)} %spans_s.1, f32[8]{0:T(128)} %decay_s.1, f32[8]{0:T(128)} %bias_s.1, f32[8]{0:T(128)} %skip_s.1, bf16[1024,512]{1,0:T(8,128)(2,1)} %x_hbm.1, bf16[1024,512]{1,0:T(8,128)(2,1)} %gate_hbm.1, ...), custom_call_target="tpu_custom_call" | custom-call | flops 10000000000 | bytes 24000000 | tf_op jit(solution)/shard_map/mixer/pallas_call | solution.py:443
  78.2 1.9 %copy.18 = bf16[1024,256]{1,0:T(8,128)(2,1)} copy(bf16[1024,256]{1,0:T(8,128)(2,1)} %get-tuple-element.8) | data formatting | bytes 1048576
  80.0 2.3 %copy.19 = f32[2,8,64,256]{3,2,1,0:T(8,128)} copy(f32[2,8,64,256]{3,2,1,0:T(8,128)} %bitcast.5) | data formatting | bytes 2097152

commit v3 on v2

--- a/solution.py
+++ b/solution.py
@@ -7,12 +7,10 @@
 
 SPAN = 128
 CAP = 6
-ORDER = (
-    (2, 0), (2, 1), (0, 2), (1, 2), (2, 2), (2, 3), (3, 2), (1, 3),
-    (3, 0), (3, 1), (0, 3), (1, 0), (1, 1), (3, 3), (0, 1), (0, 0),
-)
+UNITS = ((2, 1), (3, 1), (0, 1), (1, 1), (2, 0), (3, 0), (1, 0), (0, 0))
 SIDE = 4
 CHUNKS = 4
+WEIGHTS_FIRST = False
 BLOCKS = 8
 MESH = pl.DeviceIdType.MESH
 BF16 = jnp.bfloat16
@@ -43,7 +41,7 @@
     x_v, gate_v, step_v, sp_v, gain_v, res, cache_v,
     req_v, rreq, req_s, idx_s, pbuf, rbuf, relay,
     e_v, f_v, em_v, sel_v, yi_v, ee_v, u_v, c_v, h_v, hb_v, ssa, ss_in,
-    w_own, w_part, g_own, g_part, s1, own1, r1o, r1n, s2, acc, r2o, r2n,
+    w_all, g_all, scale_v, s1, own1, r1o, r1n, s2, acc, r2o, r2n,
     ss_mid, ss_core, ss_x, ss_y,
     sem_in, sem_sp, sem_req_s, sem_req_r, sem_rs, sem_st_s, sem_st_r, sem_out,
     sem_w, sem_ws, sem_wr, sem_gs, sem_gr, sem_1s, sem_1r, sem_2s, sem_2r, sem_ss, sem_sr,
@@ -86,16 +84,27 @@
         start = pl.multiple_of(b * 1024, 1024)
         return pltpu.make_async_copy(sp_hbm.at[:, pl.ds(start, 1024)], sp_v.at[b], sem_sp.at[b])
 
-    def w_local(i, dx, dy):
+    def w_local(dx, dy):
         start = pl.multiple_of(head_at(dx, dy, 0) * 256, 256)
-        return pltpu.make_async_copy(w_hbm.at[:, pl.ds(start, 256)], w_own.at[dx, dy], sem_w.at[i])
-
-    def w_remote(i, dx, dy):
+        dst = w_all.at[dx, pl.ds(0, 512), pl.ds(dy * 256, 256)]
+        return pltpu.make_async_copy(w_hbm.at[:, pl.ds(start, 256)], dst, sem_w.at[dx, dy])
+
+    def w_remote(dx, dy):
         start = pl.multiple_of(head_at(dx, dy, 1) * 256, 256)
-        return remote(w_hbm.at[:, pl.ds(start, 256)], w_part.at[dx, dy], sem_ws.at[i], sem_wr.at[i], partner)
+        dst = w_all.at[dx, pl.ds(512, 512), pl.ds(dy * 256, 256)]
+        return remote(w_hbm.at[:, pl.ds(start, 256)], dst, sem_ws.at[dx, dy], sem_wr.at[dx, dy], partner)
+
+    def start_weights():
+        for dx, dh in UNITS:
+            for dy in (2 * dh, 2 * dh + 1):
+                w_remote(dx, dy).start()
+                w_local(dx, dy).start()
+        loads[5].start()
 
     def g_remote(c):
-        return remote(g_own.at[c], g_part.at[c], sem_gs.at[c], sem_gr.at[c], partner)
+        return remote(
+            g_all.at[c, :, pl.ds(0, 512)], g_all.at[c, :, pl.ds(512, 512)], sem_gs.at[c], sem_gr.at[c], partner
+        )
 
     for load in loads[:5]:
         load.start()
@@ -129,11 +138,8 @@
     pl.semaphore_wait(barrier, 10)
     for k in (1, 0, 2):
         req_copy(k).start()
-    for i, (dx, dy) in enumerate(ORDER):
-        w_local(i, dx, dy).start()
-    for i, (dx, dy) in enumerate(ORDER):
-        w_remote(i, dx, dy).start()
-    loads[5].start()
+    if WEIGHTS_FIRST:
+        start_weights()
 
     sub = lax.broadcasted_iota(I32, (8, 128), 0)
     bias = jnp.zeros((8, 128), F32)
@@ -185,6 +191,8 @@
             if k == 1 and r == 2:
                 state_copy(0).start()
         state_copy((2, 1, 3)[k]).start()
+    if not WEIGHTS_FIRST:
+        start_weights()
 
     pick = me // 4
     sel_v[...] = jnp.where(
@@ -249,7 +257,7 @@
             gate = gate_v[pl.ds(pl.multiple_of(b * SPAN, SPAN), SPAN), :].astype(F32)
             gated = y * (gate / (1.0 + jnp.exp(-gate)))
             ssa[...] = jnp.where(square1 == b, jnp.sum(gated * gated, axis=1, keepdims=True), ssa[...])
-            g_own[c, s * SPAN:(s + 1) * SPAN, :] = (gated * gain_v[...]).astype(BF16)
+            g_all[c, s * SPAN:(s + 1) * SPAN, :512] = (gated * gain_v[...]).astype(BF16)
         g_remote(c).start()
 
     final_copy = pltpu.make_async_copy(h_v, state_out, sem_out)
@@ -298,25 +306,27 @@
     def stage_project(c):
         g_remote(c).wait_recv()
         done = set()
-        for i, (dx, dy) in enumerate(ORDER):
+        for dx, dh in UNITS:
             @pl.when(c == 0)
             def _():
-                w_local(i, dx, dy).wait()
-                w_remote(i, dx, dy).wait_recv()
-            term = jnp.dot(g_own[c], w_own[dx, dy], preferred_element_type=F32)
-            term += jnp.dot(g_part[c], w_part[dx, dy], preferred_element_type=F32)
-            for part, dp, dq in ((0, dx, dy), (1, dy, dx)):
-                piece = term[part * SPAN:(part + 1) * SPAN]
-                columns = pl.ds((dq % 2) * 256, 256)
-                if dp == 0:
-                    own1[part, c, dq // 2, :, columns] = piece
-                else:
-                    s1[part, c, dp - 1, dq // 2, :, columns] = piece.astype(BF16)
-                done.add((part, dp, dq))
-                pair = (part, dp, dq - dq % 2), (part, dp, dq - dq % 2 + 1)
-                kind = IMMEDIATE.get((dp, dq // 2))
-                if kind is not None and pair[0] in done and pair[1] in done:
-                    first(part, c, kind).start()
+                for dy in (2 * dh, 2 * dh + 1):
+                    w_local(dx, dy).wait()
+                    w_remote(dx, dy).wait_recv()
+            term = jnp.dot(g_all[c], w_all[dx, :, dh * 512:(dh + 1) * 512], preferred_element_type=F32)
+            for dy in (2 * dh, 2 * dh + 1):
+                for part, dp, dq in ((0, dx, dy), (1, dy, dx)):
+                    piece = term[part * SPAN:(part + 1) * SPAN, (dy % 2) * 256:(dy % 2 + 1) * 256]
+                    columns = pl.ds((dq % 2) * 256, 256)
+                    if dp == 0:
+                        own1[part, c, dq // 2, :, columns] = piece
+                    else:
+                        s1[part, c, dp - 1, dq // 2, :, columns] = piece.astype(BF16)
+            for dy in (2 * dh, 2 * dh + 1):
+                for part, dp, dq in ((0, dx, dy), (1, dy, dx)):
+                    done.add((part, dp, dq))
+                    kind = IMMEDIATE.get((dp, dq // 2))
+                    if kind is not None and (part, dp, dq ^ 1) in done:
+                        first(part, c, kind).start()
 
     def stage_pass1(c):
         for part in (0, 1):
@@ -364,6 +374,13 @@
                     r2n[part, c, 0, half].astype(F32) + r2n[part, c, 1, half].astype(F32)
                 )
 
+    def finish(c):
+        for part in (0, 1):
+            b = part * CHUNKS + c
+            rows = pl.ds(pl.multiple_of(b * SPAN, SPAN), SPAN)
+            scale = jnp.sum(jnp.where(square1 == b, scale_v[...], 0.0), axis=1, keepdims=True)
+            out[rows, :] = (res[rows, :].astype(F32) + acc[part, c] * scale).astype(BF16)
+
     def step(t, _):
         @pl.when(t < CHUNKS - 1)
         def _():
@@ -398,24 +415,24 @@
             @pl.when(jnp.logical_and(t >= lag, t < CHUNKS + lag))
             def _():
                 stage(t - lag)
+
+        @pl.when(t == 5)
+        def _():
+            for k in range(3):
+                ss_y_copy(k).wait()
+            loads[5].wait()
+            total = ss_mid[1] + ss_y[0] + ss_y[1] + ss_y[2]
+            scale = lax.rsqrt(total / 16384.0 + 1e-05)
+            scale_v[...] = jnp.transpose(jnp.concatenate([scale] * 16, axis=0))
+            finish(0)
+
+        @pl.when(t >= 5)
+        def _():
+            finish(t - 4)
         return 0
 
     stage_states(0)
     lax.fori_loop(0, CHUNKS + 4, step, 0)
-    loads[5].wait()
-
-    for k in range(3):
-        ss_y_copy(k).wait()
-    total = ss_mid[1] + ss_y[0] + ss_y[1] + ss_y[2]
-    scale = lax.rsqrt(total / 16384.0 + 1e-05)
-    scale = jnp.transpose(jnp.concatenate([scale] * 16, axis=0))
-    for part in (0, 1):
-        for c in range(CHUNKS):
-            block = part * CHUNKS + c
-            rows = pl.ds(block * SPAN, SPAN)
-            out[rows, :] = (
-                res[rows, :].astype(F32) + acc[part, c] * scale[:, block:block + 1]
-            ).astype(BF16)
 
     def drain(c, _):
         for part in (0, 1):
@@ -426,8 +443,9 @@
         return 0
 
     lax.fori_loop(0, CHUNKS, drain, 0)
-    for i, (dx, dy) in enumerate(ORDER):
-        w_remote(i, dx, dy).wait_send()
+    for dx, dh in UNITS:
+        for dy in (2 * dh, 2 * dh + 1):
+            w_remote(dx, dy).wait_send()
     for k in range(3):
         req_copy(k).wait_send()
     for i in range(6):
@@ -475,10 +493,9 @@
             pltpu.VMEM((2, 512, 256), BF16),
             pltpu.VMEM((128, 128), F32),
             pltpu.VMEM((8, 128), F32),
-            pltpu.VMEM((4, 4, 512, 256), BF16),
-            pltpu.VMEM((4, 4, 512, 256), BF16),
-            pltpu.VMEM((4, 256, 512), BF16),
-            pltpu.VMEM((4, 256, 512), BF16),
+            pltpu.VMEM((4, 1024, 1024), BF16),
+            pltpu.VMEM((4, 256, 1024), BF16),
+            pltpu.VMEM((128, 128), F32),
             pltpu.VMEM((2, 4, 3, 2, 128, 512), BF16),
             pltpu.VMEM((2, 4, 2, 128, 512), F32),
             pltpu.VMEM((2, 4, 2, 128, 512), BF16),
@@ -492,7 +509,7 @@
             pltpu.VMEM((3, 8, 128), F32),
             pltpu.VMEM((3, 8, 128), F32),
             dma((6,)), dma((8,)), dma((3,)), dma((3,)), dma((3,)), dma((6,)), dma((6,)), dma(()),
-            dma((16,)), dma((16,)), dma((16,)), dma((4,)), dma((4,)),
+            dma((4, 4)), dma((4, 4)), dma((4, 4)), dma((4,)), dma((4,)),
             dma((2, 4, 6)), dma((2, 4, 6)), dma((2, 4, 6)), dma((2, 4, 6)),
             dma((7,)), dma((7,)),
         ],

time: 82.5 us -> 80.7 us (0.978)
  Pallas kernels: 77.5 us -> 75.7 us
    pallas_call x1, Pallas kernels: 77.5 us -> 75.7 us  [mixer(): pl.pallas_call(mixer_kernel, out_shape=(jax.ShapeDtypeStruct(res.shape, r...]
where the time goes in v3:
time: 80.7 us; the launch traced here: 80.5 us
  Pallas kernels  75.7 us (94%)
  local copies, waits for them, and re-layouts  4.16 us (5%)
    pallas_call x1, Pallas kernels, mixer(): pl.pallas_call(mixer_kernel, out_shape=(jax.ShapeDtypeStruct(res.shape, r...  75.7 us
    unnamed x2, local copies, waits for them, and re-layouts  4.16 us

profile of v3, /device:TPU:1, one launch (start us, length us, event | category | flops | bytes accessed | tf_op | source)
XLA Modules:
  0.0 80.5 jit_solution(11289161498203155410)
XLA Ops:
  0.6 75.7 %mixer.1 = (bf16[1024,256]{1,0:T(8,128)(2,1)}, f32[2,512,256]{2,1,0:T(8,128)}) custom-call(s32[2,8]{1,0:T(2,128)} %owner_s.1, s32[2,8]{1,0:T(2,128)} %slot_s.1, s32[2]{0:T(128)} %spans_s.1, f32[8]{0:T(128)} %decay_s.1, f32[8]{0:T(128)} %bias_s.1, f32[8]{0:T(128)} %skip_s.1, bf16[1024,512]{1,0:T(8,128)(2,1)} %x_hbm.1, bf16[1024,512]{1,0:T(8,128)(2,1)} %gate_hbm.1, ...), custom_call_target="tpu_custom_call" | custom-call | flops 10000000000 | bytes 24000000 | tf_op jit(solution)/shard_map/mixer/pallas_call | solution.py:461
  76.3 1.9 %copy.18 = bf16[1024,256]{1,0:T(8,128)(2,1)} copy(bf16[1024,256]{1,0:T(8,128)(2,1)} %get-tuple-element.8) | data formatting | bytes 1048576
  78.2 2.3 %copy.19 = f32[2,8,64,256]{3,2,1,0:T(8,128)} copy(f32[2,8,64,256]{3,2,1,0:T(8,128)} %bitcast.5) | data formatting | bytes 2097152

commit v4 on v3

--- a/solution.py
+++ b/solution.py
@@ -35,15 +35,16 @@
 
 
 def mixer_kernel(
+    owner_hbm, slot_hbm, spans_hbm, decay_hbm, bias_hbm, skip_hbm,
+    x_hbm, gate_hbm, step_hbm, sp_hbm, gain_hbm, w_hbm, res_hbm, cache_hbm,
+    out, h_v,
     owner_s, slot_s, spans_s, decay_s, bias_s, skip_s,
-    x_hbm, gate_hbm, step_hbm, sp_hbm, gain_hbm, w_hbm, res_hbm, cache_hbm,
-    out, state_out,
     x_v, gate_v, step_v, sp_v, gain_v, res, cache_v,
     req_v, rreq, req_s, idx_s, pbuf, rbuf, relay,
-    e_v, f_v, em_v, sel_v, yi_v, ee_v, u_v, c_v, h_v, hb_v, ssa, ss_in,
+    e_v, f_v, em_v, sel_v, yi_v, ee_v, u_v, c_v, hb_v, ssa, ss_in,
     w_all, g_all, scale_v, s1, own1, r1o, r1n, s2, acc, r2o, r2n,
     ss_mid, ss_core, ss_x, ss_y,
-    sem_in, sem_sp, sem_req_s, sem_req_r, sem_rs, sem_st_s, sem_st_r, sem_out,
+    sem_in, sem_sp, sem_req_s, sem_req_r, sem_rs, sem_st_s, sem_st_r, sem_sc,
     sem_w, sem_ws, sem_wr, sem_gs, sem_gr, sem_1s, sem_1r, sem_2s, sem_2r, sem_ss, sem_sr,
 ):
     me = lax.axis_index("head")
@@ -106,10 +107,22 @@
             g_all.at[c, :, pl.ds(0, 512)], g_all.at[c, :, pl.ds(512, 512)], sem_gs.at[c], sem_gr.at[c], partner
         )
 
+    scalars = [
+        pltpu.make_async_copy(src, dst, sem_sc.at[i])
+        for i, (src, dst) in enumerate((
+            (owner_hbm, owner_s), (slot_hbm, slot_s), (spans_hbm, spans_s),
+            (decay_hbm, decay_s), (bias_hbm, bias_s), (skip_hbm, skip_s),
+        ))
+    ]
+    for scalar in scalars:
+        scalar.start()
     for load in loads[:5]:
         load.start()
     for b in range(BLOCKS):
         sp_copy(b).start()
+
+    for scalar in scalars:
+        scalar.wait()
 
     lane = lax.broadcasted_iota(I32, (8, 128), 1)
     request = jnp.zeros((8, 128), I32)
@@ -260,7 +273,6 @@
             g_all[c, s * SPAN:(s + 1) * SPAN, :512] = (gated * gain_v[...]).astype(BF16)
         g_remote(c).start()
 
-    final_copy = pltpu.make_async_copy(h_v, state_out, sem_out)
 
     def ss_core_copy():
         return remote(ss_in, ss_core, sem_ss.at[0], sem_sr.at[0], partner)
@@ -392,7 +404,6 @@
 
         @pl.when(t == 2)
         def _():
-            final_copy.start()
             ss_in[...] = jnp.transpose(ssa[...])[:8]
             ss_core_copy().start()
 
@@ -450,23 +461,27 @@
         req_copy(k).wait_send()
     for i in range(6):
         state_copy(i).wait_send()
-    final_copy.wait()
 
 
 def mixer(owner, slot, spans, decay, bias, skip, x, gate, step, sp, gain, w, res, cache):
     vmem = pl.BlockSpec(memory_space=pltpu.VMEM)
-    smem = pl.BlockSpec(memory_space=pltpu.SMEM)
     hbm = pl.BlockSpec(memory_space=pl.ANY)
     dma = pltpu.SemaphoreType.DMA
     return pl.pallas_call(
         mixer_kernel,
         out_shape=(
-            jax.ShapeDtypeStruct(res.shape, res.dtype),
-            jax.ShapeDtypeStruct((2, 512, 256), F32),
+            pltpu.VMEM(res.shape, res.dtype),
+            pltpu.VMEM((2, 512, 256), F32),
         ),
-        in_specs=[smem] * 6 + [hbm] * 8,
-        out_specs=(vmem, hbm),
+        in_specs=[hbm] * 14,
+        out_specs=(vmem, vmem),
         scratch_shapes=[
+            pltpu.SMEM((2, 8), I32),
+            pltpu.SMEM((2, 8), I32),
+            pltpu.SMEM((2,), I32),
+            pltpu.SMEM((8,), F32),
+            pltpu.SMEM((8,), F32),
+            pltpu.SMEM((8,), F32),
             pltpu.VMEM((1024, 512), BF16),
             pltpu.VMEM((1024, 512), BF16),
             pltpu.VMEM((8, 1024), F32),
@@ -489,7 +504,6 @@
             pltpu.VMEM((8, 128, 512), F32),
             pltpu.VMEM((8, 512, 256), F32),
             pltpu.VMEM((8, 128, 256), BF16),
-            pltpu.VMEM((2, 512, 256), F32),
             pltpu.VMEM((2, 512, 256), BF16),
             pltpu.VMEM((128, 128), F32),
             pltpu.VMEM((8, 128), F32),
@@ -508,7 +522,7 @@
             pltpu.VMEM((8, 128), F32),
             pltpu.VMEM((3, 8, 128), F32),
             pltpu.VMEM((3, 8, 128), F32),
-            dma((6,)), dma((8,)), dma((3,)), dma((3,)), dma((3,)), dma((6,)), dma((6,)), dma(()),
+            dma((6,)), dma((8,)), dma((3,)), dma((3,)), dma((3,)), dma((6,)), dma((6,)), dma((6,)),
             dma((4, 4)), dma((4, 4)), dma((4, 4)), dma((4,)), dma((4,)),
             dma((2, 4, 6)), dma((2, 4, 6)), dma((2, 4, 6)), dma((2, 4, 6)),
             dma((7,)), dma((7,)),
@@ -521,6 +535,36 @@
     )(owner, slot, spans, decay, bias, skip, x, gate, step, sp, gain, w, res, cache)
 
 
+def emit_kernel(mixed, state, mixed_out, state_out, sems):
+    copies = []
+    for i in range(4):
+        rows = pl.ds(i * 256, 256)
+        copies.append(pltpu.make_async_copy(mixed.at[rows], mixed_out.at[rows], sems.at[i]))
+        rows = pl.ds((i % 2) * 256, 256)
+        copies.append(pltpu.make_async_copy(state.at[i // 2, rows], state_out.at[i // 2, rows], sems.at[4 + i]))
+    for copy in copies:
+        copy.start()
+    for copy in copies:
+        copy.wait()
+
+
+def emit(mixed, state):
+    vmem = pl.BlockSpec(memory_space=pltpu.VMEM)
+    hbm = pl.BlockSpec(memory_space=pl.ANY)
+    return pl.pallas_call(
+        emit_kernel,
+        out_shape=(
+            jax.ShapeDtypeStruct(mixed.shape, mixed.dtype),
+            jax.ShapeDtypeStruct(state.shape, state.dtype),
+        ),
+        in_specs=[vmem] * 2,
+        out_specs=(hbm, hbm),
+        scratch_shapes=[pltpu.SemaphoreType.DMA((8,))],
+        compiler_params=pltpu.CompilerParams(vmem_limit_bytes=4 * 1024 * 1024),
+        name="emit",
+    )(mixed, state)
+
+
 def per_device(
     mixer_input, gate_input, step_raw, state_proj, decay_log, step_bias, skip_gain, norm_gain,
     out_weight, residual, new_spans, hit_owner, hit_slot, state_cache,
@@ -530,6 +574,7 @@
         mixer_input, gate_input, step_raw.T, state_proj.reshape(2, 8192, 256),
         norm_gain.reshape(1, 512), out_weight, residual, state_cache.reshape(64, 64, 256),
     )
+    mixed, final = emit(mixed, final)
     return mixed, final.reshape(2, 8, 64, 256)
 
 

time: 80.7 us -> 76.1 us (0.943)
  local copies, waits for them, and re-layouts: 4.16 us -> 0 us
    unnamed x2 -> x0, local copies, waits for them, and re-layouts: 4.16 us -> none
    pallas_call x1 -> x2, Pallas kernels: 75.7 us -> 75.4 us  [the longest x1 74.2 us: mixer(): pl.pallas_call(mixer_kernel, out_shape=(pltpu.VMEM(res.shape, res.dtype),...]
where the time goes in v4:
time: 76.1 us; the launch traced here: 76 us
  Pallas kernels  75.4 us (99%)
    pallas_call x1, Pallas kernels, mixer(): pl.pallas_call(mixer_kernel, out_shape=(pltpu.VMEM(res.shape, res.dtype),...  74.2 us

profile of v4, /device:TPU:1, one launch (start us, length us, event | category | flops | bytes accessed | tf_op | source)
XLA Modules:
  0.0 76.0 jit_solution(10034114298821407148)
XLA Ops:
  0.6 74.2 %mixer.1 = (bf16[1024,256]{1,0:T(8,128)(2,1)S(1)}, f32[2,512,256]{2,1,0:T(8,128)S(1)}) custom-call(s32[2,8]{1,0:T(2,128)} %owner_hbm.1, s32[2,8]{1,0:T(2,128)} %slot_hbm.1, s32[2]{0:T(128)} %spans_hbm.1, f32[8]{0:T(128)} %decay_hbm.1, f32[8]{0:T(128)} %bias_hbm.1, f32[8]{0:T(128)} %skip_hbm.1, bf16[1024,512]{1,0:T(8,128)(2,1)} %x_hbm.1, ...), custom_call_target="tpu_custom_call" | custom-call | flops 10000000000 | bytes 24000000 | tf_op jit(solution)/shard_map/mixer/pallas_call | solution.py:470
  74.8 1.2 %emit.1 = (bf16[1024,256]{1,0:T(8,128)(2,1)}, f32[2,512,256]{2,1,0:T(8,128)}) custom-call(bf16[1024,256]{1,0:T(8,128)(2,1)S(1)} %get-tuple-element.6.mixed, f32[2,512,256]{2,1,0:T(8,128)S(1)} %get-tuple-element.7.state), custom_call_target="tpu_custom_call" | custom-call | tf_op jit(solution)/shard_map/emit/pallas_call | solution.py:554

commit v5 on v4

--- a/solution.py
+++ b/solution.py
@@ -7,7 +7,7 @@
 
 SPAN = 128
 CAP = 6
-UNITS = ((2, 1), (3, 1), (0, 1), (1, 1), (2, 0), (3, 0), (1, 0), (0, 0))
+UNITS = ((2, 1), (2, 0), (3, 1), (3, 0), (1, 1), (0, 1), (1, 0), (0, 0))
 SIDE = 4
 CHUNKS = 4
 WEIGHTS_FIRST = False
@@ -41,7 +41,7 @@
     owner_s, slot_s, spans_s, decay_s, bias_s, skip_s,
     x_v, gate_v, step_v, sp_v, gain_v, res, cache_v,
     req_v, rreq, req_s, idx_s, pbuf, rbuf, relay,
-    e_v, f_v, em_v, sel_v, yi_v, ee_v, u_v, c_v, hb_v, ssa, ss_in,
+    e_v, f_v, em_v, sel_v, yi_v, silu_v, ee_v, u_v, c_v, hb_v, ssa, ss_in,
     w_all, g_all, scale_v, s1, own1, r1o, r1n, s2, acc, r2o, r2n,
     ss_mid, ss_core, ss_x, ss_y,
     sem_in, sem_sp, sem_req_s, sem_req_r, sem_rs, sem_st_s, sem_st_r, sem_sc,
@@ -149,7 +149,7 @@
         return remote(req_v, rreq.at[k], sem_req_s.at[k], sem_req_r.at[k], z_peers[k])
 
     pl.semaphore_wait(barrier, 10)
-    for k in (1, 0, 2):
+    for k in (0, 2, 1):
         req_copy(k).start()
     if WEIGHTS_FIRST:
         start_weights()
@@ -179,28 +179,22 @@
     em_v[...] = jnp.exp(jnp.broadcast_to(middle, (BLOCKS * 8, 128)))
     ssa[...] = jnp.zeros((SPAN, SPAN), F32)
 
-    def rank_copy(k):
-        return pltpu.make_async_copy(rreq.at[k], req_s.at[k], sem_rs.at[k])
-
     def state_copy(i):
         src, dst, way = (
-            (pbuf.at[pl.ds(6, 3)], relay.at[0], 0),
-            (pbuf.at[pl.ds(9, 3)], relay.at[1], 2),
+            (pbuf.at[pl.ds(6, 3)], rbuf.at[pl.ds(6, 3)], 1),
+            (pbuf.at[pl.ds(9, 3)], rbuf.at[pl.ds(9, 3)], 1),
             (pbuf.at[pl.ds(0, 6)], rbuf.at[pl.ds(0, 6)], 2),
             (pbuf.at[pl.ds(12, 6)], rbuf.at[pl.ds(12, 6)], 0),
-            (relay.at[0], rbuf.at[pl.ds(6, 3)], 0),
-            (relay.at[1], rbuf.at[pl.ds(9, 3)], 2),
         )[i]
         return remote(src, dst, sem_st_s.at[i], sem_st_r.at[i], z_peers[way])
 
     loads[0].wait()
-    for k in (1, 0, 2):
+    for k in (0, 2, 1):
         req_copy(k).wait_recv()
-        rank_copy(k).start()
-    for k in (1, 0, 2):
-        rank_copy(k).wait()
+        list_k = rreq[k]
         for r in range(CAP):
-            pbuf[k * CAP + r] = cache_v[req_s[k, 0, deep * 8 + r]]
+            place = jnp.sum(jnp.where(lane[:1] == deep * 8 + r, list_k[:1], 0))
+            pbuf[k * CAP + r] = cache_v[place]
             if k == 1 and r == 2:
                 state_copy(0).start()
         state_copy((2, 1, 3)[k]).start()
@@ -238,17 +232,13 @@
         scores = jnp.where(square0 >= square1, dot_nt(c_rows, b_rows), 0.0).astype(BF16)
         yi_v[b] = wide_e * jnp.dot(scores, z, preferred_element_type=F32) + skip * x
         u_v[b] = dot_tn(z, b_rows)
-
-        @pl.when(b == 2)
-        def _():
-            for i in (0, 1):
-                state_copy(i).wait_recv()
-                state_copy(4 + i).start()
+        gate = gate_v[pl.ds(pl.multiple_of(b * SPAN, SPAN), SPAN), :].astype(F32)
+        silu_v[b] = gate / (1.0 + jnp.exp(-gate))
         return 0
 
     lax.fori_loop(0, BLOCKS, prepare, 0)
 
-    for i in (2, 3, 4, 5):
+    for i in (0, 1, 2, 3):
         state_copy(i).wait_recv()
     for e in range(16):
         s, j = divmod(e, 8)
@@ -256,22 +246,29 @@
         sent = rbuf[idx_s[0, e]].astype(F32)
         h_v[s, j * 64:(j + 1) * 64, :] = jnp.where(idx_s[1, e] == 1, here, sent)
 
+    def fade_of(b, j):
+        fade = em_v[pl.ds(b * 8 + j, 1), :]
+        return jnp.concatenate([fade, fade], axis=1)
+
     def stage_states(c):
         for s in (0, 1):
             b = s * CHUNKS + c
             for j in range(8):
                 rows = slice(j * 64, (j + 1) * 64)
-                fade = em_v[pl.ds(b * 8 + j, 1), :]
-                fade = jnp.concatenate([fade, fade], axis=1)
-                faded = h_v[s, rows, :] * fade
-                hb_v[s, rows, :] = faded.astype(BF16)
-                h_v[s, rows, :] = (faded + u_v[b, rows, :]) * fade
+                hb_v[s, rows, :] = (h_v[s, rows, :] * fade_of(b, j)).astype(BF16)
             y = yi_v[b] + ee_v[b] * dot_nt(c_v[b], hb_v[s])
-            gate = gate_v[pl.ds(pl.multiple_of(b * SPAN, SPAN), SPAN), :].astype(F32)
-            gated = y * (gate / (1.0 + jnp.exp(-gate)))
+            gated = y * silu_v[b]
+            g_all[c, s * SPAN:(s + 1) * SPAN, :512] = (gated * gain_v[...]).astype(BF16)
+            yi_v[b] = gated
+        g_remote(c).start()
+        for s in (0, 1):
+            b = s * CHUNKS + c
+            gated = yi_v[b]
             ssa[...] = jnp.where(square1 == b, jnp.sum(gated * gated, axis=1, keepdims=True), ssa[...])
-            g_all[c, s * SPAN:(s + 1) * SPAN, :512] = (gated * gain_v[...]).astype(BF16)
-        g_remote(c).start()
+            for j in range(8):
+                rows = slice(j * 64, (j + 1) * 64)
+                fade = fade_of(b, j)
+                h_v[s, rows, :] = (h_v[s, rows, :] * fade + u_v[b, rows, :]) * fade
 
 
     def ss_core_copy():
@@ -298,11 +295,18 @@
             src, dst, way = s1.at[part, c, 2, 1], r1n.at[part, c, 1, 1], 1
         return remote(src, dst, sem_1s.at[part, c, kind], sem_1r.at[part, c, kind], p_side[part][way])
 
+    def second_to(part, c, way):
+        if way < 2:
+            return q_side[part][way]
+        near = q_side[part][way - 2]["head"]
+        far = (y_peers, x_peers)[part][1]["head"]
+        return at_head(jnp.where(c == CHUNKS - 1, far, near))
+
     def second(part, c, kind):
         if kind == 0:
-            src, dst, way = s2.at[part, c, 1, 0], r2o.at[part, c, 0], 0
+            src, dst, way = s2.at[part, c, 1, 0], r2o.at[part, c, 0], 2
         elif kind == 1:
-            src, dst, way = s2.at[part, c, 1, 1], r2o.at[part, c, 1], 1
+            src, dst, way = s2.at[part, c, 1, 1], r2o.at[part, c, 1], 3
         elif kind == 2:
             src, dst, way = s2.at[part, c, 0, 1], r2n.at[part, c, 0, 1], 0
         elif kind == 3:
@@ -311,7 +315,7 @@
             src, dst, way = s2.at[part, c, 0, 0], r2n.at[part, c, 0, 0], 0
         else:
             src, dst, way = s2.at[part, c, 2, 1], r2n.at[part, c, 1, 1], 1
-        return remote(src, dst, sem_2s.at[part, c, kind], sem_2r.at[part, c, kind], q_side[part][way])
+        return remote(src, dst, sem_2s.at[part, c, kind], sem_2r.at[part, c, kind], second_to(part, c, way))
 
     IMMEDIATE = {(2, 0): 0, (2, 1): 1, (1, 1): 2, (3, 0): 3}
 
@@ -350,34 +354,49 @@
 
     def stage_turn(c):
         for part in (0, 1):
-            sums = [None, None]
-            for half in (1, 0):
-                first(part, c, 2 if half else 4).wait_recv()
-                first(part, c, 5 if half else 3).wait_recv()
-                sums[half] = own1[part, c, half] + r1n[part, c, 0, half].astype(F32) + r1n[part, c, 1, half].astype(F32)
-                if half:
-                    s2[part, c, 1, 0] = sums[1][:64, :256].astype(BF16)
-                    second(part, c, 0).start()
-                    s2[part, c, 1, 1] = sums[1][64:, :256].astype(BF16)
-                    second(part, c, 1).start()
-                    s2[part, c, 2, 0] = sums[1][:64, 256:].astype(BF16)
-                    second(part, c, 3).start()
-                    s2[part, c, 2, 1] = sums[1][64:, 256:].astype(BF16)
-                else:
-                    s2[part, c, 0, 1] = sums[0][64:, 256:].astype(BF16)
-                    second(part, c, 2).start()
-                    s2[part, c, 0, 0] = sums[0][:64, 256:].astype(BF16)
-                    acc[part, c] = sums[0][:, :256]
+            first(part, c, 2).wait_recv()
+            first(part, c, 5).wait_recv()
+            total = own1[part, c, 1] + r1n[part, c, 0, 1].astype(F32) + r1n[part, c, 1, 1].astype(F32)
+            s2[part, c, 1, 0] = total[:64, :256].astype(BF16)
+            second(part, c, 0).start()
+            s2[part, c, 1, 1] = total[64:, :256].astype(BF16)
+            second(part, c, 1).start()
+            s2[part, c, 2, 0] = total[:64, 256:].astype(BF16)
+            second(part, c, 3).start()
+            s2[part, c, 2, 1] = total[64:, 256:].astype(BF16)
+        for part in (0, 1):
+            first(part, c, 4).wait_recv()
+            first(part, c, 3).wait_recv()
+            total = own1[part, c, 0] + r1n[part, c, 0, 0].astype(F32) + r1n[part, c, 1, 0].astype(F32)
+            s2[part, c, 0, 1] = total[64:, 256:].astype(BF16)
+            second(part, c, 2).start()
+            s2[part, c, 0, 0] = total[:64, 256:].astype(BF16)
+            acc[part, c] = total[:, :256]
+
+        @pl.when(c == CHUNKS - 1)
+        def _():
+            for part in (0, 1):
+                second(part, c, 4).start()
+                second(part, c, 5).start()
 
     def stage_pass2(c):
-        for part in (0, 1):
-            for way, (dp, half) in enumerate(((0, 0), (2, 1))):
-                second(part, c, way).wait_recv()
-                total = s2[part, c, dp, half].astype(F32) + r2o[part, c, way].astype(F32)
-                s2[part, c, dp, half] = total.astype(BF16)
-                second(part, c, 4 + way).start()
+        @pl.when(c < CHUNKS - 1)
+        def _():
+            for part in (0, 1):
+                for way, (dp, half) in enumerate(((0, 0), (2, 1))):
+                    second(part, c, way).wait_recv()
+                    total = s2[part, c, dp, half].astype(F32) + r2o[part, c, way].astype(F32)
+                    s2[part, c, dp, half] = total.astype(BF16)
+                    second(part, c, 4 + way).start()
 
     def stage_last(c):
+        @pl.when(c == CHUNKS - 1)
+        def _():
+            for part in (0, 1):
+                for half in (0, 1):
+                    second(part, c, half).wait_recv()
+                    acc[part, c, pl.ds(half * 64, 64)] += r2o[part, c, half].astype(F32)
+
         for part in (0, 1):
             for half in (0, 1):
                 second(part, c, 2 if half else 4).wait_recv()
@@ -393,6 +412,28 @@
             scale = jnp.sum(jnp.where(square1 == b, scale_v[...], 0.0), axis=1, keepdims=True)
             out[rows, :] = (res[rows, :].astype(F32) + acc[part, c] * scale).astype(BF16)
 
+    def drain_first(c):
+        for part in (0, 1):
+            for kind in range(6):
+                first(part, c, kind).wait_send()
+        g_remote(c).wait_send()
+
+    def drain_second(c):
+        @pl.when(c < CHUNKS - 1)
+        def _():
+            for part in (0, 1):
+                for kind in range(6):
+                    second(part, c, kind).wait_send()
+
+    def drain_rest():
+        for dx, dh in UNITS:
+            for dy in (2 * dh, 2 * dh + 1):
+                w_remote(dx, dy).wait_send()
+        for k in range(3):
+            req_copy(k).wait_send()
+        for i in range(4):
+            state_copy(i).wait_send()
+
     def step(t, _):
         @pl.when(t < CHUNKS - 1)
         def _():
@@ -422,12 +463,16 @@
             for k in range(3):
                 ss_y_copy(k).start()
 
-        for lag, stage in ((1, stage_pass1), (2, stage_turn), (3, stage_pass2), (4, stage_last)):
+        @pl.when(t == 4)
+        def _():
+            drain_rest()
+
+        for lag, stage in ((2, stage_pass1), (3, stage_turn), (4, stage_pass2), (5, stage_last), (5, drain_first), (6, drain_second)):
             @pl.when(jnp.logical_and(t >= lag, t < CHUNKS + lag))
             def _():
                 stage(t - lag)
 
-        @pl.when(t == 5)
+        @pl.when(t == 6)
         def _():
             for k in range(3):
                 ss_y_copy(k).wait()
@@ -437,30 +482,17 @@
             scale_v[...] = jnp.transpose(jnp.concatenate([scale] * 16, axis=0))
             finish(0)
 
-        @pl.when(t >= 5)
-        def _():
-            finish(t - 4)
+        @pl.when(t >= 6)
+        def _():
+            finish(t - 5)
         return 0
 
     stage_states(0)
-    lax.fori_loop(0, CHUNKS + 4, step, 0)
-
-    def drain(c, _):
-        for part in (0, 1):
-            for kind in range(6):
-                first(part, c, kind).wait_send()
-                second(part, c, kind).wait_send()
-        g_remote(c).wait_send()
-        return 0
-
-    lax.fori_loop(0, CHUNKS, drain, 0)
-    for dx, dh in UNITS:
-        for dy in (2 * dh, 2 * dh + 1):
-            w_remote(dx, dy).wait_send()
-    for k in range(3):
-        req_copy(k).wait_send()
-    for i in range(6):
-        state_copy(i).wait_send()
+    lax.fori_loop(0, CHUNKS + 5, step, 0)
+
+    for part in (0, 1):
+        for kind in range(6):
+            second(part, CHUNKS - 1, kind).wait_send()
 
 
 def mixer(owner, slot, spans, decay, bias, skip, x, gate, step, sp, gain, w, res, cache):
@@ -502,6 +534,7 @@
             pltpu.VMEM((128, 1024), BF16),
             pltpu.VMEM((8, 128, 512), F32),
             pltpu.VMEM((8, 128, 512), F32),
+            pltpu.VMEM((8, 128, 512), F32),
             pltpu.VMEM((8, 512, 256), F32),
             pltpu.VMEM((8, 128, 256), BF16),
             pltpu.VMEM((2, 512, 256), BF16),
@@ -522,13 +555,13 @@
             pltpu.VMEM((8, 128), F32),
             pltpu.VMEM((3, 8, 128), F32),
             pltpu.VMEM((3, 8, 128), F32),
-            dma((6,)), dma((8,)), dma((3,)), dma((3,)), dma((3,)), dma((6,)), dma((6,)), dma((6,)),
+            dma((6,)), dma((8,)), dma((3,)), dma((3,)), dma((3,)), dma((4,)), dma((4,)), dma((6,)),
             dma((4, 4)), dma((4, 4)), dma((4, 4)), dma((4,)), dma((4,)),
             dma((2, 4, 6)), dma((2, 4, 6)), dma((2, 4, 6)), dma((2, 4, 6)),
             dma((7,)), dma((7,)),
         ],
         compiler_params=pltpu.CompilerParams(
-            collective_id=0, has_side_effects=True, vmem_limit_bytes=62 * 1024 * 1024
+            collective_id=0, has_side_effects=True, vmem_limit_bytes=61 * 1024 * 1024
         ),
         cost_estimate=pl.CostEstimate(flops=10000000000, bytes_accessed=24000000, transcendentals=0),
         name="mixer",

time: 76.1 us -> 75.3 us (0.989)
  Pallas kernels: 75.4 us -> 74.6 us
    pallas_call x1, Pallas kernels: 74.2 us -> 73.4 us  [mixer(): pl.pallas_call(mixer_kernel, out_shape=(pltpu.VMEM(res.shape, res.dtype),...]
where the time goes in v5:
time: 75.3 us; the launch traced here: 75.2 us
  Pallas kernels  74.6 us (99%)
    pallas_call x1, Pallas kernels, mixer(): pl.pallas_call(mixer_kernel, out_shape=(pltpu.VMEM(res.shape, res.dtype),...  73.4 us

profile of v5, /device:TPU:1, one launch (start us, length us, event | category | flops | bytes accessed | tf_op | source)
XLA Modules:
  0.0 75.2 jit_solution(11206435722350122080)
XLA Ops:
  0.6 73.4 %mixer.1 = (bf16[1024,256]{1,0:T(8,128)(2,1)S(1)}, f32[2,512,256]{2,1,0:T(8,128)S(1)}) custom-call(s32[2,8]{1,0:T(2,128)} %owner_hbm.1, s32[2,8]{1,0:T(2,128)} %slot_hbm.1, s32[2]{0:T(128)} %spans_hbm.1, f32[8]{0:T(128)} %decay_hbm.1, f32[8]{0:T(128)} %bias_hbm.1, f32[8]{0:T(128)} %skip_hbm.1, bf16[1024,512]{1,0:T(8,128)(2,1)} %x_hbm.1, ...), custom_call_target="tpu_custom_call" | custom-call | flops 10000000000 | bytes 24000000 | tf_op jit(solution)/shard_map/mixer/pallas_call | solution.py:502
  74.0 1.2 %emit.1 = (bf16[1024,256]{1,0:T(8,128)(2,1)}, f32[2,512,256]{2,1,0:T(8,128)}) custom-call(bf16[1024,256]{1,0:T(8,128)(2,1)S(1)} %get-tuple-element.6.mixed, f32[2,512,256]{2,1,0:T(8,128)S(1)} %get-tuple-element.7.state), custom_call_target="tpu_custom_call" | custom-call | tf_op jit(solution)/shard_map/emit/pallas_call | solution.py:587

commit v6 on v5

--- a/solution.py
+++ b/solution.py
@@ -121,28 +121,18 @@
     for b in range(BLOCKS):
         sp_copy(b).start()
 
-    for scalar in scalars:
+    for scalar in scalars[:2]:
         scalar.wait()
 
     lane = lax.broadcasted_iota(I32, (8, 128), 1)
+    lane_owner = lane // 8
+    lane_rank = lane % 8
     request = jnp.zeros((8, 128), I32)
-    seen = jnp.zeros((8, 128), I32)
-    counts = [jnp.int32(0)] * 4
     for e in range(16):
         s, j = divmod(e, 8)
-        owner = owner_s[s, j]
-        place = slot_s[s, j] * 8 + j
-        named = (lane // 8) == owner
-        request = jnp.where(jnp.logical_and(named, seen == lane % 8), place, request)
-        seen = seen + jnp.where(named, 1, 0)
-        rank = jnp.int32(0)
-        for q in range(4):
-            rank = jnp.where(owner == q, counts[q], rank)
-            counts[q] = counts[q] + jnp.where(owner == q, 1, 0)
-        away = lax.rem(owner - deep + 4, 4)
-        idx_s[0, e] = jnp.where(away == 0, 0, (away - 1) * CAP + jnp.minimum(rank, CAP - 1))
-        idx_s[1, e] = jnp.where(away == 0, 1, 0)
-        idx_s[2, e] = place
+        named = lane_owner == owner_s[s, j]
+        request = jnp.where(jnp.logical_and(named, lane_rank == 0), slot_s[s, j] * 8 + j, request)
+        lane_rank = lane_rank - jnp.where(named, 1, 0)
     req_v[...] = request
 
     def req_copy(k):
@@ -153,6 +143,9 @@
         req_copy(k).start()
     if WEIGHTS_FIRST:
         start_weights()
+
+    for scalar in scalars[2:]:
+        scalar.wait()
 
     sub = lax.broadcasted_iota(I32, (8, 128), 0)
     bias = jnp.zeros((8, 128), F32)
@@ -201,6 +194,19 @@
     if not WEIGHTS_FIRST:
         start_weights()
 
+    counts = [jnp.int32(0)] * 4
+    for e in range(16):
+        s, j = divmod(e, 8)
+        owner = owner_s[s, j]
+        rank = jnp.int32(0)
+        for q in range(4):
+            rank = jnp.where(owner == q, counts[q], rank)
+            counts[q] = counts[q] + jnp.where(owner == q, 1, 0)
+        away = lax.rem(owner - deep + 4, 4)
+        idx_s[0, e] = jnp.where(away == 0, 0, (away - 1) * CAP + jnp.minimum(rank, CAP - 1))
+        idx_s[1, e] = jnp.where(away == 0, 1, 0)
+        idx_s[2, e] = slot_s[s, j] * 8 + j
+
     pick = me // 4
     sel_v[...] = jnp.where(
         lax.broadcasted_iota(I32, (SPAN, 1024), 1) == lax.broadcasted_iota(I32, (SPAN, 1024), 0) * 8 + pick, 1.0, 0.0
@@ -238,22 +244,25 @@
 
     lax.fori_loop(0, BLOCKS, prepare, 0)
 
+    def fade_of(b, j):
+        fade = em_v[pl.ds(b * 8 + j, 1), :]
+        return jnp.concatenate([fade, fade], axis=1)
+
     for i in (0, 1, 2, 3):
         state_copy(i).wait_recv()
     for e in range(16):
         s, j = divmod(e, 8)
         here = cache_v[idx_s[2, e]].astype(F32)
         sent = rbuf[idx_s[0, e]].astype(F32)
-        h_v[s, j * 64:(j + 1) * 64, :] = jnp.where(idx_s[1, e] == 1, here, sent)
-
-    def fade_of(b, j):
-        fade = em_v[pl.ds(b * 8 + j, 1), :]
-        return jnp.concatenate([fade, fade], axis=1)
-
-    def stage_states(c):
+        state = jnp.where(idx_s[1, e] == 1, here, sent)
+        rows = slice(j * 64, (j + 1) * 64)
+        h_v[s, rows, :] = state
+        hb_v[s, rows, :] = (state * fade_of(s * CHUNKS, j)).astype(BF16)
+
+    def stage_states(c, fresh=False):
         for s in (0, 1):
             b = s * CHUNKS + c
-            for j in range(8):
+            for j in range(0 if fresh else 8):
                 rows = slice(j * 64, (j + 1) * 64)
                 hb_v[s, rows, :] = (h_v[s, rows, :] * fade_of(b, j)).astype(BF16)
             y = yi_v[b] + ee_v[b] * dot_nt(c_v[b], hb_v[s])
@@ -319,10 +328,23 @@
 
     IMMEDIATE = {(2, 0): 0, (2, 1): 1, (1, 1): 2, (3, 0): 3}
 
+    def stage_pass1(c):
+        for part in (0, 1):
+            for way, (dp, half) in enumerate(((0, 0), (2, 1))):
+                first(part, c, way).wait_recv()
+                total = s1[part, c, dp, half].astype(F32) + r1o[part, c, way].astype(F32)
+                s1[part, c, dp, half] = total.astype(BF16)
+                first(part, c, 4 + way).start()
+
     def stage_project(c):
         g_remote(c).wait_recv()
         done = set()
-        for dx, dh in UNITS:
+        for unit, (dx, dh) in enumerate(UNITS):
+            if unit == 5:
+                @pl.when(c >= 1)
+                def _():
+                    stage_pass1(c - 1)
+
             @pl.when(c == 0)
             def _():
                 for dy in (2 * dh, 2 * dh + 1):
@@ -344,14 +366,6 @@
                     if kind is not None and (part, dp, dq ^ 1) in done:
                         first(part, c, kind).start()
 
-    def stage_pass1(c):
-        for part in (0, 1):
-            for way, (dp, half) in enumerate(((0, 0), (2, 1))):
-                first(part, c, way).wait_recv()
-                total = s1[part, c, dp, half].astype(F32) + r1o[part, c, way].astype(F32)
-                s1[part, c, dp, half] = total.astype(BF16)
-                first(part, c, 4 + way).start()
-
     def stage_turn(c):
         for part in (0, 1):
             first(part, c, 2).wait_recv()
@@ -467,12 +481,16 @@
         def _():
             drain_rest()
 
-        for lag, stage in ((2, stage_pass1), (3, stage_turn), (4, stage_pass2), (5, stage_last), (5, drain_first), (6, drain_second)):
+        @pl.when(t == CHUNKS)
+        def _():
+            stage_pass1(CHUNKS - 1)
+
+        for lag, stage in ((2, stage_turn), (3, stage_pass2), (4, stage_last), (4, drain_first), (5, drain_second)):
             @pl.when(jnp.logical_and(t >= lag, t < CHUNKS + lag))
             def _():
                 stage(t - lag)
 
-        @pl.when(t == 6)
+        @pl.when(t == 5)
         def _():
             for k in range(3):
                 ss_y_copy(k).wait()
@@ -482,13 +500,13 @@
             scale_v[...] = jnp.transpose(jnp.concatenate([scale] * 16, axis=0))
             finish(0)
 
-        @pl.when(t >= 6)
-        def _():
-            finish(t - 5)
+        @pl.when(t >= 5)
+        def _():
+            finish(t - 4)
         return 0
 
-    stage_states(0)
-    lax.fori_loop(0, CHUNKS + 5, step, 0)
+    stage_states(0, True)
+    lax.fori_loop(0, CHUNKS + 4, step, 0)
 
     for part in (0, 1):
         for kind in range(6):

time: 75.3 us -> 74.5 us (0.989)
  Pallas kernels: 74.6 us -> 73.7 us
    pallas_call x1, Pallas kernels: 73.4 us -> 72.5 us  [mixer(): pl.pallas_call(mixer_kernel, out_shape=(pltpu.VMEM(res.shape, res.dtype),...]
where the time goes in v6:
time: 74.5 us; the launch traced here: 74.4 us
  Pallas kernels  73.7 us (99%)
    pallas_call x1, Pallas kernels, mixer(): pl.pallas_call(mixer_kernel, out_shape=(pltpu.VMEM(res.shape, res.dtype),...  72.5 us

profile of v6, /device:TPU:1, one launch (start us, length us, event | category | flops | bytes accessed | tf_op | source)
XLA Modules:
  0.0 74.4 jit_solution(17559748644349990586)
XLA Ops:
  0.6 72.5 %mixer.1 = (bf16[1024,256]{1,0:T(8,128)(2,1)S(1)}, f32[2,512,256]{2,1,0:T(8,128)S(1)}) custom-call(s32[2,8]{1,0:T(2,128)} %owner_hbm.1, s32[2,8]{1,0:T(2,128)} %slot_hbm.1, s32[2]{0:T(128)} %spans_hbm.1, f32[8]{0:T(128)} %decay_hbm.1, f32[8]{0:T(128)} %bias_hbm.1, f32[8]{0:T(128)} %skip_hbm.1, bf16[1024,512]{1,0:T(8,128)(2,1)} %x_hbm.1, ...), custom_call_target="tpu_custom_call" | custom-call | flops 10000000000 | bytes 24000000 | tf_op jit(solution)/shard_map/mixer/pallas_call | solution.py:520
  73.2 1.2 %emit.1 = (bf16[1024,256]{1,0:T(8,128)(2,1)}, f32[2,512,256]{2,1,0:T(8,128)}) custom-call(bf16[1024,256]{1,0:T(8,128)(2,1)S(1)} %get-tuple-element.6.mixed, f32[2,512,256]{2,1,0:T(8,128)S(1)} %get-tuple-element.7.state), custom_call_target="tpu_custom_call" | custom-call | tf_op jit(solution)/shard_map/emit/pallas_call | solution.py:605

commit v7 on v6

--- a/solution.py
+++ b/solution.py
@@ -340,7 +340,7 @@
         g_remote(c).wait_recv()
         done = set()
         for unit, (dx, dh) in enumerate(UNITS):
-            if unit == 5:
+            if unit == 4:
                 @pl.when(c >= 1)
                 def _():
                     stage_pass1(c - 1)
@@ -587,12 +587,10 @@
 
 
 def emit_kernel(mixed, state, mixed_out, state_out, sems):
-    copies = []
-    for i in range(4):
-        rows = pl.ds(i * 256, 256)
-        copies.append(pltpu.make_async_copy(mixed.at[rows], mixed_out.at[rows], sems.at[i]))
-        rows = pl.ds((i % 2) * 256, 256)
-        copies.append(pltpu.make_async_copy(state.at[i // 2, rows], state_out.at[i // 2, rows], sems.at[4 + i]))
+    copies = [
+        pltpu.make_async_copy(state, state_out, sems.at[0]),
+        pltpu.make_async_copy(mixed, mixed_out, sems.at[1]),
+    ]
     for copy in copies:
         copy.start()
     for copy in copies:

time: 74.5 us -> 74.5 us (level)
  no operation moved by 1% of the time
where the time goes in v7:
time: 74.5 us; the launch traced here: 74.4 us
  Pallas kernels  73.7 us (99%)
    pallas_call x1, Pallas kernels, mixer(): pl.pallas_call(mixer_kernel, out_shape=(pltpu.VMEM(res.shape, res.dtype),...  72.5 us

profile of v7, /device:TPU:1, one launch (start us, length us, event | category | flops | bytes accessed | tf_op | source)
XLA Modules:
  0.0 74.4 jit_solution(18190631385619394196)
XLA Ops:
  0.6 72.5 %mixer.1 = (bf16[1024,256]{1,0:T(8,128)(2,1)S(1)}, f32[2,512,256]{2,1,0:T(8,128)S(1)}) custom-call(s32[2,8]{1,0:T(2,128)} %owner_hbm.1, s32[2,8]{1,0:T(2,128)} %slot_hbm.1, s32[2]{0:T(128)} %spans_hbm.1, f32[8]{0:T(128)} %decay_hbm.1, f32[8]{0:T(128)} %bias_hbm.1, f32[8]{0:T(128)} %skip_hbm.1, bf16[1024,512]{1,0:T(8,128)(2,1)} %x_hbm.1, ...), custom_call_target="tpu_custom_call" | custom-call | flops 10000000000 | bytes 24000000 | tf_op jit(solution)/shard_map/mixer/pallas_call | solution.py:520
  73.2 1.2 %emit.1 = (bf16[1024,256]{1,0:T(8,128)(2,1)}, f32[2,512,256]{2,1,0:T(8,128)}) custom-call(bf16[1024,256]{1,0:T(8,128)(2,1)S(1)} %get-tuple-element.6.mixed, f32[2,512,256]{2,1,0:T(8,128)S(1)} %get-tuple-element.7.state), custom_call_target="tpu_custom_call" | custom-call | tf_op jit(solution)/shard_map/emit/pallas_call | solution.py:603
